TPU v7x, 256 devices: a whole 4x4x8 slice. The times are simulated.
256 devices in a mesh: ctx: 32 (over x_hi, z, core), head: 8 (over y, x_lo).
Axes of the slice: x: 4 (x_hi: 2, x_lo: 2; x = x_hi * 2 + x_lo), y: 4, z: 8, core: 2. Of those that a mesh axis runs over, the one named last changes fastest.
Arguments:
- queries: bfloat16 [4, 2048, 8192], P(None, 'ctx', 'head'), as said below
- key_vectors: bfloat16 [4, 2048, 1024], P(None, 'ctx', 'head'), as said below
- value_vectors: bfloat16 [4, 2048, 1024], P(None, 'ctx', 'head'), may hold values from -6 to 6
- output_gradient: bfloat16 [4, 2048, 8192], P(None, 'ctx', 'head'), may hold values from -6 to 6
- positions: int32 [4, 2048], P(None, 'ctx'), may hold values from 0 to 2047, as said below
- segments: int32 [4, 2048], P(None, 'ctx'), may hold values from 0 to 7, as said below
Outputs:
- query_grad: bfloat16 [4, 2048, 8192], P(None, ('ctx', 'head'))
- key_gradient: bfloat16 [4, 2048, 1024], P(None, ('ctx', 'head'))
- value_gradient: bfloat16 [4, 2048, 1024], P(None, ('ctx', 'head'))
Inputs may be any that keep to these rules, and one draw needn't show every extreme that they name: `positions`: in each window each position appears in exactly one row. `segments`: in each window documents are runs of consecutive positions numbered in order of position, and every id of the range is used. `queries`: real-valued. `key_vectors`: real-valued.
All inputs are finite; a program needn't handle non-finite values.
Results may differ from a plain program's by a relative error of at most 0.012.
Values may be sent and summed in bfloat16 or wider, within the bound.
No kernel may reach another device: no remote copies, remote signals or barrier semaphores. Data moves between devices by JAX's collectives and lax.ppermute only.
A program may use at most 64 MiB of HBM per device.

v0:
```python
import math
import jax
import jax.numpy as jnp
from jax import lax
from jax.sharding import PartitionSpec as P

QUERY_HEADS = 64
KEY_VALUE_HEADS = 8
HEAD_SIZE = 128
NEG_BIG = -1e30


def passed_along(array, axis, by):
    count = lax.axis_size(axis)
    return lax.ppermute(array, axis, [(i, (i + by) % count) for i in range(count)])


def block_scores(query_four_axes, key_block, key_pos, key_seg, query_pos, query_seg):
    key_per_head = key_block.shape[1] // HEAD_SIZE
    key_three = key_block.reshape(key_block.shape[0], key_per_head, HEAD_SIZE)
    scores = jnp.einsum(
        "tkgd,skd->kgts", query_four_axes, key_three, preferred_element_type=jnp.float32
    ) * (1.0 / math.sqrt(HEAD_SIZE))
    allowed = (query_seg[:, None] == key_seg[None, :]) & (key_pos[None, :] <= query_pos[:, None])
    return (jnp.where(allowed, scores, NEG_BIG), allowed, key_three)


def stats_update(state_now, pieces, query_four_axes, grad_four, query_pos, query_seg):
    running_max, running_sum, running_dot = state_now
    key_block, value_block, key_pos, key_seg = pieces
    scores, allowed, key_three = block_scores(
        query_four_axes, key_block, key_pos, key_seg, query_pos, query_seg
    )
    value_three = value_block.reshape(key_three.shape)
    softmax_grad = jnp.einsum(
        "tkgd,skd->kgts", grad_four, value_three, preferred_element_type=jnp.float32
    )
    new_max = jnp.maximum(running_max, jnp.max(scores, axis=-1, keepdims=True))
    rescale = jnp.exp(running_max - new_max)
    weights = jnp.where(allowed, jnp.exp(scores - new_max), 0.0)
    new_sum = running_sum * rescale + jnp.sum(weights, axis=-1, keepdims=True)
    new_dot = running_dot * rescale + jnp.sum(weights * softmax_grad, axis=-1, keepdims=True)
    return (new_max, new_sum, new_dot)


def block_grads(pieces, query_four_axes, grad_four, logsum, row_delta, query_pos, query_seg):
    key_block, value_block, key_pos, key_seg = pieces
    key_rows = key_block.shape[0]
    factor = 1.0 / math.sqrt(HEAD_SIZE)
    scores, allowed, key_three = block_scores(
        query_four_axes, key_block, key_pos, key_seg, query_pos, query_seg
    )
    value_three = value_block.reshape(key_three.shape)
    softmax_out = jnp.where(allowed, jnp.exp(scores - logsum), 0.0)
    softmax_grad = jnp.einsum(
        "tkgd,skd->kgts", grad_four, value_three, preferred_element_type=jnp.float32
    )
    score_grad = softmax_out * (softmax_grad - row_delta)
    softmax_low = softmax_out.astype(jnp.bfloat16)
    score_low = score_grad.astype(jnp.bfloat16)
    value_part = jnp.einsum(
        "kgts,tkgd->skd", softmax_low, grad_four, preferred_element_type=jnp.float32
    ).reshape(key_rows, key_block.shape[1])
    key_part = (
        jnp.einsum(
            "kgts,tkgd->skd", score_low, query_four_axes, preferred_element_type=jnp.float32
        ).reshape(key_rows, key_block.shape[1])
        * factor
    )
    query_part = (
        jnp.einsum("kgts,skd->tkgd", score_low, key_three, preferred_element_type=jnp.float32)
        * factor
    )
    return (query_part, key_part, value_part)


def on_device(queries, key_vectors, value_vectors, output_gradient, positions, segments):
    window_count = queries.shape[0]
    row_count = queries.shape[1]
    query_groups = QUERY_HEADS // KEY_VALUE_HEADS
    key_width = key_vectors.shape[2]
    key_per_head = key_width // HEAD_SIZE
    query_five = queries.reshape(window_count, row_count, key_per_head, query_groups, HEAD_SIZE)
    grad_five = output_gradient.reshape(
        window_count, row_count, key_per_head, query_groups, HEAD_SIZE
    )
    stat_shape = (window_count, key_per_head, query_groups, row_count, 1)
    start_stats = (
        jnp.full(stat_shape, NEG_BIG, jnp.float32),
        jnp.zeros(stat_shape, jnp.float32),
        jnp.zeros(stat_shape, jnp.float32),
    )
    query_zero = jnp.zeros(query_five.shape, jnp.float32)
    stats_many = jax.vmap(stats_update)
    grads_many = jax.vmap(block_grads)
    gathered = (
        lax.all_gather(key_vectors, "ctx", axis=1, tiled=True),
        lax.all_gather(value_vectors, "ctx", axis=1, tiled=True),
        lax.all_gather(positions, "ctx", axis=1, tiled=True),
        lax.all_gather(segments, "ctx", axis=1, tiled=True),
    )
    whole_rows = gathered[0].shape[1]
    per_block = row_count * math.gcd(lax.axis_size("ctx"), max(1, 512 // row_count))
    block_count = whole_rows // per_block
    blocked = tuple(
        (
            jnp.moveaxis(
                member.reshape((window_count, block_count, per_block) + member.shape[2:]), 1, 0
            )
            for member in gathered
        )
    )

    def stats_step(state_now, pieces):
        return (stats_many(state_now, pieces, query_five, grad_five, positions, segments), None)

    (running_max, running_sum, running_dot), unused = lax.scan(stats_step, start_stats, blocked)
    logsum = running_max + jnp.log(running_sum)
    row_delta = running_dot / running_sum
    circle_size = lax.axis_size("ctx")
    own_index = lax.axis_index("ctx")
    key_zero = jnp.zeros(key_vectors.shape, jnp.float32)

    def cycle_turn(turn_index, cycle_state):
        query_acc, key_acc, value_acc = cycle_state
        source = (own_index - turn_index) % circle_size
        start_row = source * row_count
        pieces = tuple(
            (lax.dynamic_slice_in_dim(member, start_row, row_count, 1) for member in gathered)
        )
        query_part, key_part, value_part = grads_many(
            pieces, query_five, grad_five, logsum, row_delta, positions, segments
        )
        key_acc, value_acc = passed_along((key_acc + key_part, value_acc + value_part), "ctx", 1)
        return (query_acc + query_part, key_acc, value_acc)

    query_acc, key_acc, value_acc = lax.fori_loop(
        0, circle_size, cycle_turn, (query_zero, key_zero, key_zero)
    )
    query_low = query_acc.reshape(window_count, row_count, queries.shape[2]).astype(jnp.bfloat16)
    key_low = key_acc.astype(jnp.bfloat16)
    value_low = value_acc.astype(jnp.bfloat16)
    query_grad, key_gradient, value_gradient = (
        lax.all_to_all(query_low, "head", split_axis=1, concat_axis=2, tiled=True),
        lax.all_to_all(key_low, "head", split_axis=1, concat_axis=2, tiled=True),
        lax.all_to_all(value_low, "head", split_axis=1, concat_axis=2, tiled=True),
    )
    return (query_grad, key_gradient, value_gradient)


def solution(mesh):
    return jax.shard_map(
        on_device,
        mesh=mesh,
        in_specs=(
            P(None, "ctx", "head"),
            P(None, "ctx", "head"),
            P(None, "ctx", "head"),
            P(None, "ctx", "head"),
            P(None, "ctx"),
            P(None, "ctx"),
        ),
        out_specs=(
            P(None, ("ctx", "head"), None),
            P(None, ("ctx", "head"), None),
            P(None, ("ctx", "head"), None),
        ),
        check_vma=False,
    )
```

profile of v0, /device:TPU:2, one launch (start us, length us, event | category | flops | bytes accessed | tf_op | source)
XLA Modules:
  0.0 674.8 jit_solution(3938459747164289178)
XLA Ops:
  11.3 44.0 %all-gather = s32[32,64,4]{1,2,0:T(4,128)S(1)} all-gather(s32[1,64,4]{1,2,0:T(4,128)S(1)} %bitcast.257), channel_id=1, replica_groups=mesh['ctx'=32,'head'=8] {'ctx'}, dimensions={0}, use_global_device_ids=true | all-gather | bytes 33792 | tf_op jit(solution)/shard_map/all_gather | solution.py:100
  55.3 37.0 %all-gather.1 = s32[32,64,4]{1,2,0:T(4,128)S(1)} all-gather(s32[1,64,4]{1,2,0:T(4,128)S(1)} %bitcast.258), channel_id=1, replica_groups=mesh['ctx'=32,'head'=8] {'ctx'}, dimensions={0}, use_global_device_ids=true | all-gather | bytes 33792 | tf_op jit(solution)/shard_map/all_gather | solution.py:99
  92.9 3.1 copy.81
  96.1 76.3 %all-gather.5.cloned.1.call-done = bf16[4,2048,128]{2,1,0:T(8,128)(2,1)} async-done(((bf16[4,64,128]{2,1,0:T(8,128)(2,1)}), bf16[4,2048,128]{2,1,0:T(8,128)(2,1)}) %all-gather.5.cloned.1.call-update) | async-done | bytes 2097168 | tf_op jit(solution)/shard_map/all_gather | solution.py:97
  172.4 3.2 copy.82
  175.6 42.4 %while.35 = (s32[]{:T(128)}, f32[4,1,8,64,1]{3,2,0,4,1:T(8,128)S(1)}, f32[4,1,8,64,1]{3,2,0,4,1:T(8,128)S(1)}, f32[4,1,8,64,1]{3,2,0,4,1:T(8,128)S(1)}, s32[4,64...) while((s32[]{:T(128)}, ...), condition=%wide.region_4.5_spmd.clone, body=%wide.region_0.4_spmd.clone.sunk | while | flops 551958528 | bytes 32181424 | solution.py:117
  175.8 3.8 fusion.66
  179.5 3.7 fusion.68
  183.2 2.9 fusion.67
  186.4 3.8 fusion.66
  190.1 3.7 fusion.68
  193.8 2.9 fusion.67
  197.0 3.8 fusion.66
  200.7 3.7 fusion.68
  204.4 2.9 fusion.67
  207.6 3.8 fusion.66
  211.4 3.7 fusion.68
  215.1 2.9 fusion.67
  218.1 415.3 %while.36 = (s32[]{:T(128)}, f32[4,64,1,8,128]{4,1,3,0,2:T(8,128)S(1)}, f32[4,64,128]{2,1,0:T(8,128)S(1)}, f32[4,64,128]{2,1,0:T(8,128)S(1)}, s32[]{:T(128)}, /*...) while((s32[]{:T(128)}, ...), condition=%wide.region_6.7_spmd.clone, body=%wide.region_5.6_spmd.clone.sunk | while | flops 169754640 | bytes 8380878 | solution.py:137
  224.2 5.4 collective-permute-done
  231.3 1.5 fusion.79
  236.4 6.3 collective-permute-done
  249.3 6.3 collective-permute-done
  262.3 6.3 collective-permute-done
  270.2 1.5 fusion.79
  275.3 6.3 collective-permute-done
  283.2 1.5 fusion.79
  288.3 6.3 collective-permute-done
  296.2 1.5 fusion.79
  301.2 6.3 collective-permute-done
  309.2 1.5 fusion.79
  314.2 6.3 collective-permute-done
  322.1 1.5 fusion.79
  327.2 6.3 collective-permute-done
  335.1 1.5 fusion.79
  340.2 6.3 collective-permute-done
  353.2 6.3 collective-permute-done
  366.1 6.3 collective-permute-done
  379.1 6.3 collective-permute-done
  392.1 6.3 collective-permute-done
  405.1 6.3 collective-permute-done
  418.0 6.3 collective-permute-done
  431.0 6.3 collective-permute-done
  444.0 6.3 collective-permute-done
  457.0 6.3 collective-permute-done
  469.9 6.3 collective-permute-done
  482.9 6.3 collective-permute-done
  495.9 6.3 collective-permute-done
  508.9 6.3 collective-permute-done
  521.9 6.3 collective-permute-done
  534.8 6.3 collective-permute-done
  547.8 6.3 collective-permute-done
  560.8 6.3 collective-permute-done
  573.8 6.3 collective-permute-done
  586.7 6.3 collective-permute-done
  599.7 6.3 collective-permute-done
  612.7 6.3 collective-permute-done
  625.7 6.3 collective-permute-done
  634.1 5.7 all-to-all-start.2
  640.5 4.3 all-to-all-done.2
  644.9 4.5 all-to-all-start.1
  650.8 4.7 all-to-all-done.1
  655.5 4.0 all-to-all-start
  660.8 6.3 all-to-all-done
  (373 shorter events, 213.1 us)
Async XLA Ops:
  7.2 85.8 %all-gather.7.cloned.1.call-start = ((), (), s32[]{:S(2)}) async-start(), calls=%async_computation.4 | async-start | bytes 2162688 | tf_op jit(solution)/shard_map/all_gather | solution.py:98
  7.9 164.5 %all-gather.5.cloned.1.call-start = ((), (), s32[]{:S(2)}) async-start(), calls=%async_computation.3 | async-start | bytes 2162688 | tf_op jit(solution)/shard_map/all_gather | solution.py:97
  221.6 8.1 %collective-permute-start = (f32[4,64,128]{2,1,0:T(8,128)S(1)}, f32[4,64,128]{2,1,0:T(8,128)S(1)}, u32[]{:S(2)}, u32[]{:S(2)}) collective-permute-start(f32[4,64,128]{2,1,0:T(8,128)S(1)} %fusion.82), channel_id=1, source_target_pairs={{0,8},{8,16},{16,24},{24,32},{32,40},{40,48},{48,56},{56,64},{64,7... | collective-permute-start | bytes 393224 | tf_op jit(solution)/shard_map/while/body/eval_jaxpr/ppermute | solution.py:15
  222.2 8.9 %collective-permute-start.1 = (f32[4,64,128]{2,1,0:T(8,128)S(1)}, f32[4,64,128]{2,1,0:T(8,128)S(1)}, u32[]{:S(2)}, u32[]{:S(2)}) collective-permute-start(f32[4,64,128]{2,1,0:T(8,128)S(1)} %fusion.83), channel_id=1, source_target_pairs={{0,8},{8,16},{16,24},{24,32},{32,40},{40,48},{48,56},{56,64},{64,7... | collective-permute-start | bytes 393224 | tf_op jit(solution)/shard_map/while/body/eval_jaxpr/ppermute | solution.py:15
  234.6 8.1 %collective-permute-start = (f32[4,64,128]{2,1,0:T(8,128)S(1)}, f32[4,64,128]{2,1,0:T(8,128)S(1)}, u32[]{:S(2)}, u32[]{:S(2)}) collective-permute-start(f32[4,64,128]{2,1,0:T(8,128)S(1)} %fusion.82), channel_id=1, source_target_pairs={{0,8},{8,16},{16,24},{24,32},{32,40},{40,48},{48,56},{56,64},{64,7... | collective-permute-start | bytes 393224 | tf_op jit(solution)/shard_map/while/body/eval_jaxpr/ppermute | solution.py:15
  234.9 9.1 %collective-permute-start.1 = (f32[4,64,128]{2,1,0:T(8,128)S(1)}, f32[4,64,128]{2,1,0:T(8,128)S(1)}, u32[]{:S(2)}, u32[]{:S(2)}) collective-permute-start(f32[4,64,128]{2,1,0:T(8,128)S(1)} %fusion.83), channel_id=1, source_target_pairs={{0,8},{8,16},{16,24},{24,32},{32,40},{40,48},{48,56},{56,64},{64,7... | collective-permute-start | bytes 393224 | tf_op jit(solution)/shard_map/while/body/eval_jaxpr/ppermute | solution.py:15
  247.5 8.1 %collective-permute-start = (f32[4,64,128]{2,1,0:T(8,128)S(1)}, f32[4,64,128]{2,1,0:T(8,128)S(1)}, u32[]{:S(2)}, u32[]{:S(2)}) collective-permute-start(f32[4,64,128]{2,1,0:T(8,128)S(1)} %fusion.82), channel_id=1, source_target_pairs={{0,8},{8,16},{16,24},{24,32},{32,40},{40,48},{48,56},{56,64},{64,7... | collective-permute-start | bytes 393224 | tf_op jit(solution)/shard_map/while/body/eval_jaxpr/ppermute | solution.py:15
  247.9 9.1 %collective-permute-start.1 = (f32[4,64,128]{2,1,0:T(8,128)S(1)}, f32[4,64,128]{2,1,0:T(8,128)S(1)}, u32[]{:S(2)}, u32[]{:S(2)}) collective-permute-start(f32[4,64,128]{2,1,0:T(8,128)S(1)} %fusion.83), channel_id=1, source_target_pairs={{0,8},{8,16},{16,24},{24,32},{32,40},{40,48},{48,56},{56,64},{64,7... | collective-permute-start | bytes 393224 | tf_op jit(solution)/shard_map/while/body/eval_jaxpr/ppermute | solution.py:15
  260.5 8.1 %collective-permute-start = (f32[4,64,128]{2,1,0:T(8,128)S(1)}, f32[4,64,128]{2,1,0:T(8,128)S(1)}, u32[]{:S(2)}, u32[]{:S(2)}) collective-permute-start(f32[4,64,128]{2,1,0:T(8,128)S(1)} %fusion.82), channel_id=1, source_target_pairs={{0,8},{8,16},{16,24},{24,32},{32,40},{40,48},{48,56},{56,64},{64,7... | collective-permute-start | bytes 393224 | tf_op jit(solution)/shard_map/while/body/eval_jaxpr/ppermute | solution.py:15
  260.9 9.1 %collective-permute-start.1 = (f32[4,64,128]{2,1,0:T(8,128)S(1)}, f32[4,64,128]{2,1,0:T(8,128)S(1)}, u32[]{:S(2)}, u32[]{:S(2)}) collective-permute-start(f32[4,64,128]{2,1,0:T(8,128)S(1)} %fusion.83), channel_id=1, source_target_pairs={{0,8},{8,16},{16,24},{24,32},{32,40},{40,48},{48,56},{56,64},{64,7... | collective-permute-start | bytes 393224 | tf_op jit(solution)/shard_map/while/body/eval_jaxpr/ppermute | solution.py:15
  273.5 8.1 %collective-permute-start = (f32[4,64,128]{2,1,0:T(8,128)S(1)}, f32[4,64,128]{2,1,0:T(8,128)S(1)}, u32[]{:S(2)}, u32[]{:S(2)}) collective-permute-start(f32[4,64,128]{2,1,0:T(8,128)S(1)} %fusion.82), channel_id=1, source_target_pairs={{0,8},{8,16},{16,24},{24,32},{32,40},{40,48},{48,56},{56,64},{64,7... | collective-permute-start | bytes 393224 | tf_op jit(solution)/shard_map/while/body/eval_jaxpr/ppermute | solution.py:15
  273.9 9.1 %collective-permute-start.1 = (f32[4,64,128]{2,1,0:T(8,128)S(1)}, f32[4,64,128]{2,1,0:T(8,128)S(1)}, u32[]{:S(2)}, u32[]{:S(2)}) collective-permute-start(f32[4,64,128]{2,1,0:T(8,128)S(1)} %fusion.83), channel_id=1, source_target_pairs={{0,8},{8,16},{16,24},{24,32},{32,40},{40,48},{48,56},{56,64},{64,7... | collective-permute-start | bytes 393224 | tf_op jit(solution)/shard_map/while/body/eval_jaxpr/ppermute | solution.py:15
  286.5 8.1 %collective-permute-start = (f32[4,64,128]{2,1,0:T(8,128)S(1)}, f32[4,64,128]{2,1,0:T(8,128)S(1)}, u32[]{:S(2)}, u32[]{:S(2)}) collective-permute-start(f32[4,64,128]{2,1,0:T(8,128)S(1)} %fusion.82), channel_id=1, source_target_pairs={{0,8},{8,16},{16,24},{24,32},{32,40},{40,48},{48,56},{56,64},{64,7... | collective-permute-start | bytes 393224 | tf_op jit(solution)/shard_map/while/body/eval_jaxpr/ppermute | solution.py:15
  286.9 9.1 %collective-permute-start.1 = (f32[4,64,128]{2,1,0:T(8,128)S(1)}, f32[4,64,128]{2,1,0:T(8,128)S(1)}, u32[]{:S(2)}, u32[]{:S(2)}) collective-permute-start(f32[4,64,128]{2,1,0:T(8,128)S(1)} %fusion.83), channel_id=1, source_target_pairs={{0,8},{8,16},{16,24},{24,32},{32,40},{40,48},{48,56},{56,64},{64,7... | collective-permute-start | bytes 393224 | tf_op jit(solution)/shard_map/while/body/eval_jaxpr/ppermute | solution.py:15
  299.4 8.1 %collective-permute-start = (f32[4,64,128]{2,1,0:T(8,128)S(1)}, f32[4,64,128]{2,1,0:T(8,128)S(1)}, u32[]{:S(2)}, u32[]{:S(2)}) collective-permute-start(f32[4,64,128]{2,1,0:T(8,128)S(1)} %fusion.82), channel_id=1, source_target_pairs={{0,8},{8,16},{16,24},{24,32},{32,40},{40,48},{48,56},{56,64},{64,7... | collective-permute-start | bytes 393224 | tf_op jit(solution)/shard_map/while/body/eval_jaxpr/ppermute | solution.py:15
  299.8 9.1 %collective-permute-start.1 = (f32[4,64,128]{2,1,0:T(8,128)S(1)}, f32[4,64,128]{2,1,0:T(8,128)S(1)}, u32[]{:S(2)}, u32[]{:S(2)}) collective-permute-start(f32[4,64,128]{2,1,0:T(8,128)S(1)} %fusion.83), channel_id=1, source_target_pairs={{0,8},{8,16},{16,24},{24,32},{32,40},{40,48},{48,56},{56,64},{64,7... | collective-permute-start | bytes 393224 | tf_op jit(solution)/shard_map/while/body/eval_jaxpr/ppermute | solution.py:15
  312.4 8.1 %collective-permute-start = (f32[4,64,128]{2,1,0:T(8,128)S(1)}, f32[4,64,128]{2,1,0:T(8,128)S(1)}, u32[]{:S(2)}, u32[]{:S(2)}) collective-permute-start(f32[4,64,128]{2,1,0:T(8,128)S(1)} %fusion.82), channel_id=1, source_target_pairs={{0,8},{8,16},{16,24},{24,32},{32,40},{40,48},{48,56},{56,64},{64,7... | collective-permute-start | bytes 393224 | tf_op jit(solution)/shard_map/while/body/eval_jaxpr/ppermute | solution.py:15
  312.8 9.1 %collective-permute-start.1 = (f32[4,64,128]{2,1,0:T(8,128)S(1)}, f32[4,64,128]{2,1,0:T(8,128)S(1)}, u32[]{:S(2)}, u32[]{:S(2)}) collective-permute-start(f32[4,64,128]{2,1,0:T(8,128)S(1)} %fusion.83), channel_id=1, source_target_pairs={{0,8},{8,16},{16,24},{24,32},{32,40},{40,48},{48,56},{56,64},{64,7... | collective-permute-start | bytes 393224 | tf_op jit(solution)/shard_map/while/body/eval_jaxpr/ppermute | solution.py:15
  325.4 8.1 %collective-permute-start = (f32[4,64,128]{2,1,0:T(8,128)S(1)}, f32[4,64,128]{2,1,0:T(8,128)S(1)}, u32[]{:S(2)}, u32[]{:S(2)}) collective-permute-start(f32[4,64,128]{2,1,0:T(8,128)S(1)} %fusion.82), channel_id=1, source_target_pairs={{0,8},{8,16},{16,24},{24,32},{32,40},{40,48},{48,56},{56,64},{64,7... | collective-permute-start | bytes 393224 | tf_op jit(solution)/shard_map/while/body/eval_jaxpr/ppermute | solution.py:15
  325.8 9.1 %collective-permute-start.1 = (f32[4,64,128]{2,1,0:T(8,128)S(1)}, f32[4,64,128]{2,1,0:T(8,128)S(1)}, u32[]{:S(2)}, u32[]{:S(2)}) collective-permute-start(f32[4,64,128]{2,1,0:T(8,128)S(1)} %fusion.83), channel_id=1, source_target_pairs={{0,8},{8,16},{16,24},{24,32},{32,40},{40,48},{48,56},{56,64},{64,7... | collective-permute-start | bytes 393224 | tf_op jit(solution)/shard_map/while/body/eval_jaxpr/ppermute | solution.py:15
  338.4 8.1 %collective-permute-start = (f32[4,64,128]{2,1,0:T(8,128)S(1)}, f32[4,64,128]{2,1,0:T(8,128)S(1)}, u32[]{:S(2)}, u32[]{:S(2)}) collective-permute-start(f32[4,64,128]{2,1,0:T(8,128)S(1)} %fusion.82), channel_id=1, source_target_pairs={{0,8},{8,16},{16,24},{24,32},{32,40},{40,48},{48,56},{56,64},{64,7... | collective-permute-start | bytes 393224 | tf_op jit(solution)/shard_map/while/body/eval_jaxpr/ppermute | solution.py:15
  338.8 9.1 %collective-permute-start.1 = (f32[4,64,128]{2,1,0:T(8,128)S(1)}, f32[4,64,128]{2,1,0:T(8,128)S(1)}, u32[]{:S(2)}, u32[]{:S(2)}) collective-permute-start(f32[4,64,128]{2,1,0:T(8,128)S(1)} %fusion.83), channel_id=1, source_target_pairs={{0,8},{8,16},{16,24},{24,32},{32,40},{40,48},{48,56},{56,64},{64,7... | collective-permute-start | bytes 393224 | tf_op jit(solution)/shard_map/while/body/eval_jaxpr/ppermute | solution.py:15
  351.4 8.1 %collective-permute-start = (f32[4,64,128]{2,1,0:T(8,128)S(1)}, f32[4,64,128]{2,1,0:T(8,128)S(1)}, u32[]{:S(2)}, u32[]{:S(2)}) collective-permute-start(f32[4,64,128]{2,1,0:T(8,128)S(1)} %fusion.82), channel_id=1, source_target_pairs={{0,8},{8,16},{16,24},{24,32},{32,40},{40,48},{48,56},{56,64},{64,7... | collective-permute-start | bytes 393224 | tf_op jit(solution)/shard_map/while/body/eval_jaxpr/ppermute | solution.py:15
  351.7 9.1 %collective-permute-start.1 = (f32[4,64,128]{2,1,0:T(8,128)S(1)}, f32[4,64,128]{2,1,0:T(8,128)S(1)}, u32[]{:S(2)}, u32[]{:S(2)}) collective-permute-start(f32[4,64,128]{2,1,0:T(8,128)S(1)} %fusion.83), channel_id=1, source_target_pairs={{0,8},{8,16},{16,24},{24,32},{32,40},{40,48},{48,56},{56,64},{64,7... | collective-permute-start | bytes 393224 | tf_op jit(solution)/shard_map/while/body/eval_jaxpr/ppermute | solution.py:15
  364.3 8.1 %collective-permute-start = (f32[4,64,128]{2,1,0:T(8,128)S(1)}, f32[4,64,128]{2,1,0:T(8,128)S(1)}, u32[]{:S(2)}, u32[]{:S(2)}) collective-permute-start(f32[4,64,128]{2,1,0:T(8,128)S(1)} %fusion.82), channel_id=1, source_target_pairs={{0,8},{8,16},{16,24},{24,32},{32,40},{40,48},{48,56},{56,64},{64,7... | collective-permute-start | bytes 393224 | tf_op jit(solution)/shard_map/while/body/eval_jaxpr/ppermute | solution.py:15
  364.7 9.1 %collective-permute-start.1 = (f32[4,64,128]{2,1,0:T(8,128)S(1)}, f32[4,64,128]{2,1,0:T(8,128)S(1)}, u32[]{:S(2)}, u32[]{:S(2)}) collective-permute-start(f32[4,64,128]{2,1,0:T(8,128)S(1)} %fusion.83), channel_id=1, source_target_pairs={{0,8},{8,16},{16,24},{24,32},{32,40},{40,48},{48,56},{56,64},{64,7... | collective-permute-start | bytes 393224 | tf_op jit(solution)/shard_map/while/body/eval_jaxpr/ppermute | solution.py:15
  377.3 8.1 %collective-permute-start = (f32[4,64,128]{2,1,0:T(8,128)S(1)}, f32[4,64,128]{2,1,0:T(8,128)S(1)}, u32[]{:S(2)}, u32[]{:S(2)}) collective-permute-start(f32[4,64,128]{2,1,0:T(8,128)S(1)} %fusion.82), channel_id=1, source_target_pairs={{0,8},{8,16},{16,24},{24,32},{32,40},{40,48},{48,56},{56,64},{64,7... | collective-permute-start | bytes 393224 | tf_op jit(solution)/shard_map/while/body/eval_jaxpr/ppermute | solution.py:15
  377.7 9.1 %collective-permute-start.1 = (f32[4,64,128]{2,1,0:T(8,128)S(1)}, f32[4,64,128]{2,1,0:T(8,128)S(1)}, u32[]{:S(2)}, u32[]{:S(2)}) collective-permute-start(f32[4,64,128]{2,1,0:T(8,128)S(1)} %fusion.83), channel_id=1, source_target_pairs={{0,8},{8,16},{16,24},{24,32},{32,40},{40,48},{48,56},{56,64},{64,7... | collective-permute-start | bytes 393224 | tf_op jit(solution)/shard_map/while/body/eval_jaxpr/ppermute | solution.py:15
  390.3 8.1 %collective-permute-start = (f32[4,64,128]{2,1,0:T(8,128)S(1)}, f32[4,64,128]{2,1,0:T(8,128)S(1)}, u32[]{:S(2)}, u32[]{:S(2)}) collective-permute-start(f32[4,64,128]{2,1,0:T(8,128)S(1)} %fusion.82), channel_id=1, source_target_pairs={{0,8},{8,16},{16,24},{24,32},{32,40},{40,48},{48,56},{56,64},{64,7... | collective-permute-start | bytes 393224 | tf_op jit(solution)/shard_map/while/body/eval_jaxpr/ppermute | solution.py:15
  390.7 9.1 %collective-permute-start.1 = (f32[4,64,128]{2,1,0:T(8,128)S(1)}, f32[4,64,128]{2,1,0:T(8,128)S(1)}, u32[]{:S(2)}, u32[]{:S(2)}) collective-permute-start(f32[4,64,128]{2,1,0:T(8,128)S(1)} %fusion.83), channel_id=1, source_target_pairs={{0,8},{8,16},{16,24},{24,32},{32,40},{40,48},{48,56},{56,64},{64,7... | collective-permute-start | bytes 393224 | tf_op jit(solution)/shard_map/while/body/eval_jaxpr/ppermute | solution.py:15
  403.3 8.1 %collective-permute-start = (f32[4,64,128]{2,1,0:T(8,128)S(1)}, f32[4,64,128]{2,1,0:T(8,128)S(1)}, u32[]{:S(2)}, u32[]{:S(2)}) collective-permute-start(f32[4,64,128]{2,1,0:T(8,128)S(1)} %fusion.82), channel_id=1, source_target_pairs={{0,8},{8,16},{16,24},{24,32},{32,40},{40,48},{48,56},{56,64},{64,7... | collective-permute-start | bytes 393224 | tf_op jit(solution)/shard_map/while/body/eval_jaxpr/ppermute | solution.py:15
  403.6 9.1 %collective-permute-start.1 = (f32[4,64,128]{2,1,0:T(8,128)S(1)}, f32[4,64,128]{2,1,0:T(8,128)S(1)}, u32[]{:S(2)}, u32[]{:S(2)}) collective-permute-start(f32[4,64,128]{2,1,0:T(8,128)S(1)} %fusion.83), channel_id=1, source_target_pairs={{0,8},{8,16},{16,24},{24,32},{32,40},{40,48},{48,56},{56,64},{64,7... | collective-permute-start | bytes 393224 | tf_op jit(solution)/shard_map/while/body/eval_jaxpr/ppermute | solution.py:15
  416.2 8.1 %collective-permute-start = (f32[4,64,128]{2,1,0:T(8,128)S(1)}, f32[4,64,128]{2,1,0:T(8,128)S(1)}, u32[]{:S(2)}, u32[]{:S(2)}) collective-permute-start(f32[4,64,128]{2,1,0:T(8,128)S(1)} %fusion.82), channel_id=1, source_target_pairs={{0,8},{8,16},{16,24},{24,32},{32,40},{40,48},{48,56},{56,64},{64,7... | collective-permute-start | bytes 393224 | tf_op jit(solution)/shard_map/while/body/eval_jaxpr/ppermute | solution.py:15
  416.6 9.1 %collective-permute-start.1 = (f32[4,64,128]{2,1,0:T(8,128)S(1)}, f32[4,64,128]{2,1,0:T(8,128)S(1)}, u32[]{:S(2)}, u32[]{:S(2)}) collective-permute-start(f32[4,64,128]{2,1,0:T(8,128)S(1)} %fusion.83), channel_id=1, source_target_pairs={{0,8},{8,16},{16,24},{24,32},{32,40},{40,48},{48,56},{56,64},{64,7... | collective-permute-start | bytes 393224 | tf_op jit(solution)/shard_map/while/body/eval_jaxpr/ppermute | solution.py:15
  429.2 8.1 %collective-permute-start = (f32[4,64,128]{2,1,0:T(8,128)S(1)}, f32[4,64,128]{2,1,0:T(8,128)S(1)}, u32[]{:S(2)}, u32[]{:S(2)}) collective-permute-start(f32[4,64,128]{2,1,0:T(8,128)S(1)} %fusion.82), channel_id=1, source_target_pairs={{0,8},{8,16},{16,24},{24,32},{32,40},{40,48},{48,56},{56,64},{64,7... | collective-permute-start | bytes 393224 | tf_op jit(solution)/shard_map/while/body/eval_jaxpr/ppermute | solution.py:15
  429.6 9.1 %collective-permute-start.1 = (f32[4,64,128]{2,1,0:T(8,128)S(1)}, f32[4,64,128]{2,1,0:T(8,128)S(1)}, u32[]{:S(2)}, u32[]{:S(2)}) collective-permute-start(f32[4,64,128]{2,1,0:T(8,128)S(1)} %fusion.83), channel_id=1, source_target_pairs={{0,8},{8,16},{16,24},{24,32},{32,40},{40,48},{48,56},{56,64},{64,7... | collective-permute-start | bytes 393224 | tf_op jit(solution)/shard_map/while/body/eval_jaxpr/ppermute | solution.py:15
  442.2 8.1 %collective-permute-start = (f32[4,64,128]{2,1,0:T(8,128)S(1)}, f32[4,64,128]{2,1,0:T(8,128)S(1)}, u32[]{:S(2)}, u32[]{:S(2)}) collective-permute-start(f32[4,64,128]{2,1,0:T(8,128)S(1)} %fusion.82), channel_id=1, source_target_pairs={{0,8},{8,16},{16,24},{24,32},{32,40},{40,48},{48,56},{56,64},{64,7... | collective-permute-start | bytes 393224 | tf_op jit(solution)/shard_map/while/body/eval_jaxpr/ppermute | solution.py:15
  442.6 9.1 %collective-permute-start.1 = (f32[4,64,128]{2,1,0:T(8,128)S(1)}, f32[4,64,128]{2,1,0:T(8,128)S(1)}, u32[]{:S(2)}, u32[]{:S(2)}) collective-permute-start(f32[4,64,128]{2,1,0:T(8,128)S(1)} %fusion.83), channel_id=1, source_target_pairs={{0,8},{8,16},{16,24},{24,32},{32,40},{40,48},{48,56},{56,64},{64,7... | collective-permute-start | bytes 393224 | tf_op jit(solution)/shard_map/while/body/eval_jaxpr/ppermute | solution.py:15
  455.2 8.1 %collective-permute-start = (f32[4,64,128]{2,1,0:T(8,128)S(1)}, f32[4,64,128]{2,1,0:T(8,128)S(1)}, u32[]{:S(2)}, u32[]{:S(2)}) collective-permute-start(f32[4,64,128]{2,1,0:T(8,128)S(1)} %fusion.82), channel_id=1, source_target_pairs={{0,8},{8,16},{16,24},{24,32},{32,40},{40,48},{48,56},{56,64},{64,7... | collective-permute-start | bytes 393224 | tf_op jit(solution)/shard_map/while/body/eval_jaxpr/ppermute | solution.py:15
  455.5 9.1 %collective-permute-start.1 = (f32[4,64,128]{2,1,0:T(8,128)S(1)}, f32[4,64,128]{2,1,0:T(8,128)S(1)}, u32[]{:S(2)}, u32[]{:S(2)}) collective-permute-start(f32[4,64,128]{2,1,0:T(8,128)S(1)} %fusion.83), channel_id=1, source_target_pairs={{0,8},{8,16},{16,24},{24,32},{32,40},{40,48},{48,56},{56,64},{64,7... | collective-permute-start | bytes 393224 | tf_op jit(solution)/shard_map/while/body/eval_jaxpr/ppermute | solution.py:15
  468.1 8.1 %collective-permute-start = (f32[4,64,128]{2,1,0:T(8,128)S(1)}, f32[4,64,128]{2,1,0:T(8,128)S(1)}, u32[]{:S(2)}, u32[]{:S(2)}) collective-permute-start(f32[4,64,128]{2,1,0:T(8,128)S(1)} %fusion.82), channel_id=1, source_target_pairs={{0,8},{8,16},{16,24},{24,32},{32,40},{40,48},{48,56},{56,64},{64,7... | collective-permute-start | bytes 393224 | tf_op jit(solution)/shard_map/while/body/eval_jaxpr/ppermute | solution.py:15
  468.5 9.1 %collective-permute-start.1 = (f32[4,64,128]{2,1,0:T(8,128)S(1)}, f32[4,64,128]{2,1,0:T(8,128)S(1)}, u32[]{:S(2)}, u32[]{:S(2)}) collective-permute-start(f32[4,64,128]{2,1,0:T(8,128)S(1)} %fusion.83), channel_id=1, source_target_pairs={{0,8},{8,16},{16,24},{24,32},{32,40},{40,48},{48,56},{56,64},{64,7... | collective-permute-start | bytes 393224 | tf_op jit(solution)/shard_map/while/body/eval_jaxpr/ppermute | solution.py:15
  481.1 8.1 %collective-permute-start = (f32[4,64,128]{2,1,0:T(8,128)S(1)}, f32[4,64,128]{2,1,0:T(8,128)S(1)}, u32[]{:S(2)}, u32[]{:S(2)}) collective-permute-start(f32[4,64,128]{2,1,0:T(8,128)S(1)} %fusion.82), channel_id=1, source_target_pairs={{0,8},{8,16},{16,24},{24,32},{32,40},{40,48},{48,56},{56,64},{64,7... | collective-permute-start | bytes 393224 | tf_op jit(solution)/shard_map/while/body/eval_jaxpr/ppermute | solution.py:15
  481.5 9.1 %collective-permute-start.1 = (f32[4,64,128]{2,1,0:T(8,128)S(1)}, f32[4,64,128]{2,1,0:T(8,128)S(1)}, u32[]{:S(2)}, u32[]{:S(2)}) collective-permute-start(f32[4,64,128]{2,1,0:T(8,128)S(1)} %fusion.83), channel_id=1, source_target_pairs={{0,8},{8,16},{16,24},{24,32},{32,40},{40,48},{48,56},{56,64},{64,7... | collective-permute-start | bytes 393224 | tf_op jit(solution)/shard_map/while/body/eval_jaxpr/ppermute | solution.py:15
  494.1 8.1 %collective-permute-start = (f32[4,64,128]{2,1,0:T(8,128)S(1)}, f32[4,64,128]{2,1,0:T(8,128)S(1)}, u32[]{:S(2)}, u32[]{:S(2)}) collective-permute-start(f32[4,64,128]{2,1,0:T(8,128)S(1)} %fusion.82), channel_id=1, source_target_pairs={{0,8},{8,16},{16,24},{24,32},{32,40},{40,48},{48,56},{56,64},{64,7... | collective-permute-start | bytes 393224 | tf_op jit(solution)/shard_map/while/body/eval_jaxpr/ppermute | solution.py:15
  494.5 9.1 %collective-permute-start.1 = (f32[4,64,128]{2,1,0:T(8,128)S(1)}, f32[4,64,128]{2,1,0:T(8,128)S(1)}, u32[]{:S(2)}, u32[]{:S(2)}) collective-permute-start(f32[4,64,128]{2,1,0:T(8,128)S(1)} %fusion.83), channel_id=1, source_target_pairs={{0,8},{8,16},{16,24},{24,32},{32,40},{40,48},{48,56},{56,64},{64,7... | collective-permute-start | bytes 393224 | tf_op jit(solution)/shard_map/while/body/eval_jaxpr/ppermute | solution.py:15
  507.5 9.1 %collective-permute-start.1 = (f32[4,64,128]{2,1,0:T(8,128)S(1)}, f32[4,64,128]{2,1,0:T(8,128)S(1)}, u32[]{:S(2)}, u32[]{:S(2)}) collective-permute-start(f32[4,64,128]{2,1,0:T(8,128)S(1)} %fusion.83), channel_id=1, source_target_pairs={{0,8},{8,16},{16,24},{24,32},{32,40},{40,48},{48,56},{56,64},{64,7... | collective-permute-start | bytes 393224 | tf_op jit(solution)/shard_map/while/body/eval_jaxpr/ppermute | solution.py:15
  520.4 9.1 %collective-permute-start.1 = (f32[4,64,128]{2,1,0:T(8,128)S(1)}, f32[4,64,128]{2,1,0:T(8,128)S(1)}, u32[]{:S(2)}, u32[]{:S(2)}) collective-permute-start(f32[4,64,128]{2,1,0:T(8,128)S(1)} %fusion.83), channel_id=1, source_target_pairs={{0,8},{8,16},{16,24},{24,32},{32,40},{40,48},{48,56},{56,64},{64,7... | collective-permute-start | bytes 393224 | tf_op jit(solution)/shard_map/while/body/eval_jaxpr/ppermute | solution.py:15
  533.4 9.1 %collective-permute-start.1 = (f32[4,64,128]{2,1,0:T(8,128)S(1)}, f32[4,64,128]{2,1,0:T(8,128)S(1)}, u32[]{:S(2)}, u32[]{:S(2)}) collective-permute-start(f32[4,64,128]{2,1,0:T(8,128)S(1)} %fusion.83), channel_id=1, source_target_pairs={{0,8},{8,16},{16,24},{24,32},{32,40},{40,48},{48,56},{56,64},{64,7... | collective-permute-start | bytes 393224 | tf_op jit(solution)/shard_map/while/body/eval_jaxpr/ppermute | solution.py:15
  546.4 9.1 %collective-permute-start.1 = (f32[4,64,128]{2,1,0:T(8,128)S(1)}, f32[4,64,128]{2,1,0:T(8,128)S(1)}, u32[]{:S(2)}, u32[]{:S(2)}) collective-permute-start(f32[4,64,128]{2,1,0:T(8,128)S(1)} %fusion.83), channel_id=1, source_target_pairs={{0,8},{8,16},{16,24},{24,32},{32,40},{40,48},{48,56},{56,64},{64,7... | collective-permute-start | bytes 393224 | tf_op jit(solution)/shard_map/while/body/eval_jaxpr/ppermute | solution.py:15
  559.4 9.1 %collective-permute-start.1 = (f32[4,64,128]{2,1,0:T(8,128)S(1)}, f32[4,64,128]{2,1,0:T(8,128)S(1)}, u32[]{:S(2)}, u32[]{:S(2)}) collective-permute-start(f32[4,64,128]{2,1,0:T(8,128)S(1)} %fusion.83), channel_id=1, source_target_pairs={{0,8},{8,16},{16,24},{24,32},{32,40},{40,48},{48,56},{56,64},{64,7... | collective-permute-start | bytes 393224 | tf_op jit(solution)/shard_map/while/body/eval_jaxpr/ppermute | solution.py:15
  572.0 8.1 %collective-permute-start = (f32[4,64,128]{2,1,0:T(8,128)S(1)}, f32[4,64,128]{2,1,0:T(8,128)S(1)}, u32[]{:S(2)}, u32[]{:S(2)}) collective-permute-start(f32[4,64,128]{2,1,0:T(8,128)S(1)} %fusion.82), channel_id=1, source_target_pairs={{0,8},{8,16},{16,24},{24,32},{32,40},{40,48},{48,56},{56,64},{64,7... | collective-permute-start | bytes 393224 | tf_op jit(solution)/shard_map/while/body/eval_jaxpr/ppermute | solution.py:15
  572.3 9.1 %collective-permute-start.1 = (f32[4,64,128]{2,1,0:T(8,128)S(1)}, f32[4,64,128]{2,1,0:T(8,128)S(1)}, u32[]{:S(2)}, u32[]{:S(2)}) collective-permute-start(f32[4,64,128]{2,1,0:T(8,128)S(1)} %fusion.83), channel_id=1, source_target_pairs={{0,8},{8,16},{16,24},{24,32},{32,40},{40,48},{48,56},{56,64},{64,7... | collective-permute-start | bytes 393224 | tf_op jit(solution)/shard_map/while/body/eval_jaxpr/ppermute | solution.py:15
  584.9 8.1 %collective-permute-start = (f32[4,64,128]{2,1,0:T(8,128)S(1)}, f32[4,64,128]{2,1,0:T(8,128)S(1)}, u32[]{:S(2)}, u32[]{:S(2)}) collective-permute-start(f32[4,64,128]{2,1,0:T(8,128)S(1)} %fusion.82), channel_id=1, source_target_pairs={{0,8},{8,16},{16,24},{24,32},{32,40},{40,48},{48,56},{56,64},{64,7... | collective-permute-start | bytes 393224 | tf_op jit(solution)/shard_map/while/body/eval_jaxpr/ppermute | solution.py:15
  585.3 9.1 %collective-permute-start.1 = (f32[4,64,128]{2,1,0:T(8,128)S(1)}, f32[4,64,128]{2,1,0:T(8,128)S(1)}, u32[]{:S(2)}, u32[]{:S(2)}) collective-permute-start(f32[4,64,128]{2,1,0:T(8,128)S(1)} %fusion.83), channel_id=1, source_target_pairs={{0,8},{8,16},{16,24},{24,32},{32,40},{40,48},{48,56},{56,64},{64,7... | collective-permute-start | bytes 393224 | tf_op jit(solution)/shard_map/while/body/eval_jaxpr/ppermute | solution.py:15
  597.9 8.1 %collective-permute-start = (f32[4,64,128]{2,1,0:T(8,128)S(1)}, f32[4,64,128]{2,1,0:T(8,128)S(1)}, u32[]{:S(2)}, u32[]{:S(2)}) collective-permute-start(f32[4,64,128]{2,1,0:T(8,128)S(1)} %fusion.82), channel_id=1, source_target_pairs={{0,8},{8,16},{16,24},{24,32},{32,40},{40,48},{48,56},{56,64},{64,7... | collective-permute-start | bytes 393224 | tf_op jit(solution)/shard_map/while/body/eval_jaxpr/ppermute | solution.py:15
  598.3 9.1 %collective-permute-start.1 = (f32[4,64,128]{2,1,0:T(8,128)S(1)}, f32[4,64,128]{2,1,0:T(8,128)S(1)}, u32[]{:S(2)}, u32[]{:S(2)}) collective-permute-start(f32[4,64,128]{2,1,0:T(8,128)S(1)} %fusion.83), channel_id=1, source_target_pairs={{0,8},{8,16},{16,24},{24,32},{32,40},{40,48},{48,56},{56,64},{64,7... | collective-permute-start | bytes 393224 | tf_op jit(solution)/shard_map/while/body/eval_jaxpr/ppermute | solution.py:15
  610.9 8.1 %collective-permute-start = (f32[4,64,128]{2,1,0:T(8,128)S(1)}, f32[4,64,128]{2,1,0:T(8,128)S(1)}, u32[]{:S(2)}, u32[]{:S(2)}) collective-permute-start(f32[4,64,128]{2,1,0:T(8,128)S(1)} %fusion.82), channel_id=1, source_target_pairs={{0,8},{8,16},{16,24},{24,32},{32,40},{40,48},{48,56},{56,64},{64,7... | collective-permute-start | bytes 393224 | tf_op jit(solution)/shard_map/while/body/eval_jaxpr/ppermute | solution.py:15
  611.3 9.1 %collective-permute-start.1 = (f32[4,64,128]{2,1,0:T(8,128)S(1)}, f32[4,64,128]{2,1,0:T(8,128)S(1)}, u32[]{:S(2)}, u32[]{:S(2)}) collective-permute-start(f32[4,64,128]{2,1,0:T(8,128)S(1)} %fusion.83), channel_id=1, source_target_pairs={{0,8},{8,16},{16,24},{24,32},{32,40},{40,48},{48,56},{56,64},{64,7... | collective-permute-start | bytes 393224 | tf_op jit(solution)/shard_map/while/body/eval_jaxpr/ppermute | solution.py:15
  623.9 8.1 %collective-permute-start = (f32[4,64,128]{2,1,0:T(8,128)S(1)}, f32[4,64,128]{2,1,0:T(8,128)S(1)}, u32[]{:S(2)}, u32[]{:S(2)}) collective-permute-start(f32[4,64,128]{2,1,0:T(8,128)S(1)} %fusion.82), channel_id=1, source_target_pairs={{0,8},{8,16},{16,24},{24,32},{32,40},{40,48},{48,56},{56,64},{64,7... | collective-permute-start | bytes 393224 | tf_op jit(solution)/shard_map/while/body/eval_jaxpr/ppermute | solution.py:15
  624.2 9.1 %collective-permute-start.1 = (f32[4,64,128]{2,1,0:T(8,128)S(1)}, f32[4,64,128]{2,1,0:T(8,128)S(1)}, u32[]{:S(2)}, u32[]{:S(2)}) collective-permute-start(f32[4,64,128]{2,1,0:T(8,128)S(1)} %fusion.83), channel_id=1, source_target_pairs={{0,8},{8,16},{16,24},{24,32},{32,40},{40,48},{48,56},{56,64},{64,7... | collective-permute-start | bytes 393224 | tf_op jit(solution)/shard_map/while/body/eval_jaxpr/ppermute | solution.py:15
  634.1 10.8 %all-to-all-start.2 = ((bf16[4,64,128]{2,0,1:T(4,128)(2,1)}), bf16[4,64,128]{2,0,1:T(4,128)(2,1)S(1)}, u32[]{:S(2)}, u32[]{:S(2)}) async-start(bf16[4,64,128]{2,0,1:T(4,128)(2,1)} %copy.79), calls=%async_computation.2 | async-start | bytes 131072 | tf_op jit(solution)/shard_map/all_to_all | solution.py:146
  644.9 10.6 %all-to-all-start.1 = ((bf16[4,64,128]{2,0,1:T(4,128)(2,1)}), bf16[4,64,128]{2,0,1:T(4,128)(2,1)S(1)}, u32[]{:S(2)}, u32[]{:S(2)}) async-start(bf16[4,64,128]{2,0,1:T(4,128)(2,1)} %copy.80), calls=%async_computation.1 | async-start | bytes 131072 | tf_op jit(solution)/shard_map/all_to_all | solution.py:145
  655.5 11.6 %all-to-all-start = ((bf16[4,64,1024]{2,0,1:T(4,128)(2,1)}), bf16[4,64,1024]{2,0,1:T(4,128)(2,1)S(1)}, u32[]{:S(2)}, u32[]{:S(2)}) async-start(bf16[4,64,1024]{2,0,1:T(4,128)(2,1)} %reshape.190), calls=%async_computation | async-start | bytes 1048576 | tf_op jit(solution)/shard_map/all_to_all | solution.py:144
  (11 other events, 107.4 us)
Sparse Core Ops, SparseCore 0:
  10.8 82.0 all-gather.6
  95.8 76.5 all-gather.4
where the time goes:
time: 680 us; the launch traced here: 675 us
  waiting for transfers between devices  339 us (50%)
  matrix products  182 us (27%)
  blocking collectives  80.9 us (12%)
  starting transfers between devices  20.6 us (3%)
  other arithmetic  20 us (3%)
  local copies, waits for them, and re-layouts  16.3 us (2%)
  between operations  14.2 us (2%)
    ppermute x64, waiting for transfers between devices, passed_along(): lax.ppermute(array, axis, [(i, (i + by) % count) for i in range(count)])  245 us
    all_gather x1, waiting for transfers between devices, on_device(): lax.all_gather(key_vectors, 'ctx', axis=1, tiled=True)  76.3 us
    dot_general x36, matrix products, block_scores(): jnp.einsum('tkgd,skd->kgts', query_four_axes, key_three, preferred_elemen...  62.8 us
    dot_general x32, matrix products, block_grads(): jnp.einsum('tkgd,skd->kgts', grad_four, value_three, preferred_element_ty...  47.2 us
    all_gather x1, blocking collectives, on_device(): lax.all_gather(segments, 'ctx', axis=1, tiled=True)  44 us
    dot_general x32, matrix products, block_grads(): jnp.einsum('kgts,skd->tkgd', score_low, key_three, preferred_element_type...  41.9 us
    all_gather x1, blocking collectives, on_device(): lax.all_gather(positions, 'ctx', axis=1, tiled=True)  37 us
    reduce_sum x4, other arithmetic, stats_update(): new_sum = running_sum * rescale + jnp.sum(weights, axis=-1, keepdims=True)  14.7 us
  transfers between devices with their start and end apart: 69, of which 69 were waited for; matrix products, arithmetic and copies ran while one was open for 9% of the time, Pallas kernels for 0%

commit v1 on v0

--- a/solution.py
+++ b/solution.py
@@ -94,7 +94,9 @@
     stats_many = jax.vmap(stats_update)
     grads_many = jax.vmap(block_grads)
     gathered = (
-        lax.all_gather(key_vectors, "ctx", axis=1, tiled=True),
+        jnp.concatenate(
+            lax.all_to_all(jnp.stack([key_vectors] * lax.axis_size("ctx")), "ctx", 0, 0), axis=1
+        ),
         lax.all_gather(value_vectors, "ctx", axis=1, tiled=True),
         lax.all_gather(positions, "ctx", axis=1, tiled=True),
         lax.all_gather(segments, "ctx", axis=1, tiled=True),

time: 680 us -> 655 us (0.963)
  waiting for transfers between devices: 339 us -> 260 us
  blocking collectives: 80.9 us -> 121 us
  starting transfers between devices: 20.6 us -> 32.3 us
    all_gather x1 -> x0, waiting for transfers between devices: 76.3 us -> none  [on_device(): lax.all_gather(key_vectors, 'ctx', axis=1, tiled=True)]
    all_gather x1, blocking collectives: 37 us -> 84.3 us  [on_device(): lax.all_gather(positions, 'ctx', axis=1, tiled=True)]
    all_to_all x0 -> x1, starting transfers between devices: none -> 10.7 us  [on_device(): lax.all_to_all(jnp.stack([key_vectors] * lax.axis_size('ctx')), 'ctx', 0, 0)]
    all_gather x1, blocking collectives: 44 us -> 36.9 us  [on_device(): lax.all_gather(segments, 'ctx', axis=1, tiled=True)]
  transfers between devices with their start and end apart: 69 -> 69, of which waited for: 69 -> 67; matrix products, arithmetic and copies ran while one was open for 9% -> 9% of each run, Pallas kernels for 0% -> 0%
where the time goes in v1:
time: 655 us; the launch traced here: 649 us
  waiting for transfers between devices  260 us (40%)
  matrix products  182 us (28%)
  blocking collectives  121 us (18%)
  starting transfers between devices  32.3 us (5%)
  other arithmetic  20 us (3%)
  local copies, waits for them, and re-layouts  17 us (3%)
  between operations  14.2 us (2%)
    ppermute x64, waiting for transfers between devices, passed_along(): lax.ppermute(array, axis, [(i, (i + by) % count) for i in range(count)])  244 us
    all_gather x1, blocking collectives, on_device(): lax.all_gather(positions, 'ctx', axis=1, tiled=True)  84.3 us
    dot_general x36, matrix products, block_scores(): jnp.einsum('tkgd,skd->kgts', query_four_axes, key_three, preferred_elemen...  62.9 us
    dot_general x32, matrix products, block_grads(): jnp.einsum('tkgd,skd->kgts', grad_four, value_three, preferred_element_ty...  47.2 us
    dot_general x32, matrix products, block_grads(): jnp.einsum('kgts,skd->tkgd', score_low, key_three, preferred_element_type...  41.9 us
    all_gather x1, blocking collectives, on_device(): lax.all_gather(segments, 'ctx', axis=1, tiled=True)  36.9 us
    reduce_sum x4, other arithmetic, stats_update(): new_sum = running_sum * rescale + jnp.sum(weights, axis=-1, keepdims=True)  14.7 us
  transfers between devices with their start and end apart: 69, of which 67 were waited for; matrix products, arithmetic and copies ran while one was open for 9% of the time, Pallas kernels for 0%

profile of v1, /device:TPU:2, one launch (start us, length us, event | category | flops | bytes accessed | tf_op | source)
XLA Modules:
  0.0 649.3 jit_solution(2152304552630235395)
XLA Ops:
  7.9 2.8 stack.2
  10.7 10.7 %all-to-all-start = ((bf16[32,4,64,128]{3,2,1,0:T(8,128)(2,1)}), bf16[32,4,64,128]{3,2,1,0:T(8,128)(2,1)}, u32[]{:S(2)}, u32[]{:S(2)}) async-start(bf16[32,4,64,128]{3,2,1,0:T(8,128)(2,1)} %stack.2), calls=%async_computation | async-start | bytes 4194304 | tf_op jit(solution)/shard_map/all_to_all | solution.py:98
  21.9 84.3 %all-gather.1 = s32[32,64,4]{1,2,0:T(4,128)S(1)} all-gather(s32[1,64,4]{1,2,0:T(4,128)S(1)} %bitcast.263), channel_id=1, replica_groups=mesh['ctx'=32,'head'=8] {'ctx'}, dimensions={0}, use_global_device_ids=true | all-gather | bytes 33792 | tf_op jit(solution)/shard_map/all_gather | solution.py:101
  106.3 36.9 %all-gather = s32[32,64,4]{1,2,0:T(4,128)S(1)} all-gather(s32[1,64,4]{1,2,0:T(4,128)S(1)} %bitcast.262), channel_id=1, replica_groups=mesh['ctx'=32,'head'=8] {'ctx'}, dimensions={0}, use_global_device_ids=true | all-gather | bytes 33792 | tf_op jit(solution)/shard_map/all_gather | solution.py:102
  143.3 3.2 copy.82
  146.5 3.2 copy.45
  149.7 42.5 %while.35 = (s32[]{:T(128)}, f32[4,1,8,64,1]{3,2,0,4,1:T(8,128)S(1)}, f32[4,1,8,64,1]{3,2,0,4,1:T(8,128)S(1)}, f32[4,1,8,64,1]{3,2,0,4,1:T(8,128)S(1)}, s32[4,64...) while((s32[]{:T(128)}, ...), condition=%wide.region_4.5_spmd.clone, body=%wide.region_0.4_spmd.clone.sunk | while | flops 551958528 | bytes 32181424 | solution.py:119
  149.8 3.8 fusion.66
  153.6 3.7 fusion.68
  157.3 2.9 fusion.67
  160.5 3.8 fusion.66
  164.3 3.7 fusion.68
  168.0 2.9 fusion.67
  171.1 3.8 fusion.66
  174.9 3.7 fusion.68
  178.6 2.9 fusion.67
  181.7 3.8 fusion.66
  185.5 3.7 fusion.68
  189.2 2.9 fusion.67
  192.2 415.3 %while.36 = (s32[]{:T(128)}, f32[4,64,1,8,128]{4,1,3,0,2:T(8,128)S(1)}, f32[4,64,128]{2,1,0:T(8,128)S(1)}, f32[4,64,128]{2,1,0:T(8,128)S(1)}, s32[]{:T(128)}, /*...) while((s32[]{:T(128)}, ...), condition=%wide.region_6.7_spmd.clone, body=%wide.region_5.6_spmd.clone.sunk | while | flops 169754640 | bytes 8380878 | solution.py:139
  196.4 1.5 collective-permute-start.1
  199.3 4.6 collective-permute-done
  205.5 1.5 fusion.79
  210.5 6.3 collective-permute-done
  218.4 1.5 fusion.79
  223.5 6.3 collective-permute-done
  231.4 1.5 fusion.79
  236.5 6.3 collective-permute-done
  249.5 6.3 collective-permute-done
  262.4 6.3 collective-permute-done
  275.4 6.3 collective-permute-done
  288.4 6.3 collective-permute-done
  296.3 1.5 fusion.79
  301.4 6.3 collective-permute-done
  309.3 1.5 fusion.79
  314.3 6.3 collective-permute-done
  327.3 6.3 collective-permute-done
  340.3 6.3 collective-permute-done
  353.3 6.3 collective-permute-done
  366.3 6.3 collective-permute-done
  379.2 6.3 collective-permute-done
  392.2 6.3 collective-permute-done
  405.2 6.3 collective-permute-done
  418.2 6.3 collective-permute-done
  431.1 6.3 collective-permute-done
  444.1 6.3 collective-permute-done
  457.1 6.3 collective-permute-done
  470.1 6.3 collective-permute-done
  483.0 6.3 collective-permute-done
  496.0 6.3 collective-permute-done
  509.0 6.3 collective-permute-done
  522.0 6.3 collective-permute-done
  535.0 6.3 collective-permute-done
  547.9 6.3 collective-permute-done
  560.9 6.3 collective-permute-done
  573.9 6.3 collective-permute-done
  586.9 6.3 collective-permute-done
  599.8 6.3 collective-permute-done
  608.3 6.0 all-to-all-start.3
  614.9 4.3 all-to-all-done.3
  619.3 4.5 all-to-all-start.2
  625.2 4.7 all-to-all-done.2
  629.9 4.0 all-to-all-start.1
  635.2 6.3 all-to-all-done.1
  (377 shorter events, 212.1 us)
Async XLA Ops:
  7.2 136.1 %all-gather.4.cloned.1.call-start = ((), (), s32[]{:S(2)}) async-start(), calls=%async_computation.4 | async-start | bytes 2162688 | tf_op jit(solution)/shard_map/all_gather | solution.py:100
  10.7 135.8 %all-to-all-start = ((bf16[32,4,64,128]{3,2,1,0:T(8,128)(2,1)}), bf16[32,4,64,128]{3,2,1,0:T(8,128)(2,1)}, u32[]{:S(2)}, u32[]{:S(2)}) async-start(bf16[32,4,64,128]{3,2,1,0:T(8,128)(2,1)} %stack.2), calls=%async_computation | async-start | bytes 4194304 | tf_op jit(solution)/shard_map/all_to_all | solution.py:98
  195.8 8.1 %collective-permute-start = (f32[4,64,128]{2,1,0:T(8,128)S(1)}, f32[4,64,128]{2,1,0:T(8,128)S(1)}, u32[]{:S(2)}, u32[]{:S(2)}) collective-permute-start(f32[4,64,128]{2,1,0:T(8,128)S(1)} %fusion.82), channel_id=1, source_target_pairs={{0,8},{8,16},{16,24},{24,32},{32,40},{40,48},{48,56},{56,64},{64,7... | collective-permute-start | bytes 393224 | tf_op jit(solution)/shard_map/while/body/eval_jaxpr/ppermute | solution.py:15
  196.4 8.8 %collective-permute-start.1 = (f32[4,64,128]{2,1,0:T(8,128)S(1)}, f32[4,64,128]{2,1,0:T(8,128)S(1)}, u32[]{:S(2)}, u32[]{:S(2)}) collective-permute-start(f32[4,64,128]{2,1,0:T(8,128)S(1)} %fusion.83), channel_id=1, source_target_pairs={{0,8},{8,16},{16,24},{24,32},{32,40},{40,48},{48,56},{56,64},{64,7... | collective-permute-start | bytes 393224 | tf_op jit(solution)/shard_map/while/body/eval_jaxpr/ppermute | solution.py:15
  208.7 8.1 %collective-permute-start = (f32[4,64,128]{2,1,0:T(8,128)S(1)}, f32[4,64,128]{2,1,0:T(8,128)S(1)}, u32[]{:S(2)}, u32[]{:S(2)}) collective-permute-start(f32[4,64,128]{2,1,0:T(8,128)S(1)} %fusion.82), channel_id=1, source_target_pairs={{0,8},{8,16},{16,24},{24,32},{32,40},{40,48},{48,56},{56,64},{64,7... | collective-permute-start | bytes 393224 | tf_op jit(solution)/shard_map/while/body/eval_jaxpr/ppermute | solution.py:15
  209.1 9.1 %collective-permute-start.1 = (f32[4,64,128]{2,1,0:T(8,128)S(1)}, f32[4,64,128]{2,1,0:T(8,128)S(1)}, u32[]{:S(2)}, u32[]{:S(2)}) collective-permute-start(f32[4,64,128]{2,1,0:T(8,128)S(1)} %fusion.83), channel_id=1, source_target_pairs={{0,8},{8,16},{16,24},{24,32},{32,40},{40,48},{48,56},{56,64},{64,7... | collective-permute-start | bytes 393224 | tf_op jit(solution)/shard_map/while/body/eval_jaxpr/ppermute | solution.py:15
  221.7 8.1 %collective-permute-start = (f32[4,64,128]{2,1,0:T(8,128)S(1)}, f32[4,64,128]{2,1,0:T(8,128)S(1)}, u32[]{:S(2)}, u32[]{:S(2)}) collective-permute-start(f32[4,64,128]{2,1,0:T(8,128)S(1)} %fusion.82), channel_id=1, source_target_pairs={{0,8},{8,16},{16,24},{24,32},{32,40},{40,48},{48,56},{56,64},{64,7... | collective-permute-start | bytes 393224 | tf_op jit(solution)/shard_map/while/body/eval_jaxpr/ppermute | solution.py:15
  222.1 9.1 %collective-permute-start.1 = (f32[4,64,128]{2,1,0:T(8,128)S(1)}, f32[4,64,128]{2,1,0:T(8,128)S(1)}, u32[]{:S(2)}, u32[]{:S(2)}) collective-permute-start(f32[4,64,128]{2,1,0:T(8,128)S(1)} %fusion.83), channel_id=1, source_target_pairs={{0,8},{8,16},{16,24},{24,32},{32,40},{40,48},{48,56},{56,64},{64,7... | collective-permute-start | bytes 393224 | tf_op jit(solution)/shard_map/while/body/eval_jaxpr/ppermute | solution.py:15
  234.7 8.1 %collective-permute-start = (f32[4,64,128]{2,1,0:T(8,128)S(1)}, f32[4,64,128]{2,1,0:T(8,128)S(1)}, u32[]{:S(2)}, u32[]{:S(2)}) collective-permute-start(f32[4,64,128]{2,1,0:T(8,128)S(1)} %fusion.82), channel_id=1, source_target_pairs={{0,8},{8,16},{16,24},{24,32},{32,40},{40,48},{48,56},{56,64},{64,7... | collective-permute-start | bytes 393224 | tf_op jit(solution)/shard_map/while/body/eval_jaxpr/ppermute | solution.py:15
  235.1 9.1 %collective-permute-start.1 = (f32[4,64,128]{2,1,0:T(8,128)S(1)}, f32[4,64,128]{2,1,0:T(8,128)S(1)}, u32[]{:S(2)}, u32[]{:S(2)}) collective-permute-start(f32[4,64,128]{2,1,0:T(8,128)S(1)} %fusion.83), channel_id=1, source_target_pairs={{0,8},{8,16},{16,24},{24,32},{32,40},{40,48},{48,56},{56,64},{64,7... | collective-permute-start | bytes 393224 | tf_op jit(solution)/shard_map/while/body/eval_jaxpr/ppermute | solution.py:15
  247.7 8.1 %collective-permute-start = (f32[4,64,128]{2,1,0:T(8,128)S(1)}, f32[4,64,128]{2,1,0:T(8,128)S(1)}, u32[]{:S(2)}, u32[]{:S(2)}) collective-permute-start(f32[4,64,128]{2,1,0:T(8,128)S(1)} %fusion.82), channel_id=1, source_target_pairs={{0,8},{8,16},{16,24},{24,32},{32,40},{40,48},{48,56},{56,64},{64,7... | collective-permute-start | bytes 393224 | tf_op jit(solution)/shard_map/while/body/eval_jaxpr/ppermute | solution.py:15
  248.0 9.1 %collective-permute-start.1 = (f32[4,64,128]{2,1,0:T(8,128)S(1)}, f32[4,64,128]{2,1,0:T(8,128)S(1)}, u32[]{:S(2)}, u32[]{:S(2)}) collective-permute-start(f32[4,64,128]{2,1,0:T(8,128)S(1)} %fusion.83), channel_id=1, source_target_pairs={{0,8},{8,16},{16,24},{24,32},{32,40},{40,48},{48,56},{56,64},{64,7... | collective-permute-start | bytes 393224 | tf_op jit(solution)/shard_map/while/body/eval_jaxpr/ppermute | solution.py:15
  260.6 8.1 %collective-permute-start = (f32[4,64,128]{2,1,0:T(8,128)S(1)}, f32[4,64,128]{2,1,0:T(8,128)S(1)}, u32[]{:S(2)}, u32[]{:S(2)}) collective-permute-start(f32[4,64,128]{2,1,0:T(8,128)S(1)} %fusion.82), channel_id=1, source_target_pairs={{0,8},{8,16},{16,24},{24,32},{32,40},{40,48},{48,56},{56,64},{64,7... | collective-permute-start | bytes 393224 | tf_op jit(solution)/shard_map/while/body/eval_jaxpr/ppermute | solution.py:15
  261.0 9.1 %collective-permute-start.1 = (f32[4,64,128]{2,1,0:T(8,128)S(1)}, f32[4,64,128]{2,1,0:T(8,128)S(1)}, u32[]{:S(2)}, u32[]{:S(2)}) collective-permute-start(f32[4,64,128]{2,1,0:T(8,128)S(1)} %fusion.83), channel_id=1, source_target_pairs={{0,8},{8,16},{16,24},{24,32},{32,40},{40,48},{48,56},{56,64},{64,7... | collective-permute-start | bytes 393224 | tf_op jit(solution)/shard_map/while/body/eval_jaxpr/ppermute | solution.py:15
  273.6 8.1 %collective-permute-start = (f32[4,64,128]{2,1,0:T(8,128)S(1)}, f32[4,64,128]{2,1,0:T(8,128)S(1)}, u32[]{:S(2)}, u32[]{:S(2)}) collective-permute-start(f32[4,64,128]{2,1,0:T(8,128)S(1)} %fusion.82), channel_id=1, source_target_pairs={{0,8},{8,16},{16,24},{24,32},{32,40},{40,48},{48,56},{56,64},{64,7... | collective-permute-start | bytes 393224 | tf_op jit(solution)/shard_map/while/body/eval_jaxpr/ppermute | solution.py:15
  274.0 9.1 %collective-permute-start.1 = (f32[4,64,128]{2,1,0:T(8,128)S(1)}, f32[4,64,128]{2,1,0:T(8,128)S(1)}, u32[]{:S(2)}, u32[]{:S(2)}) collective-permute-start(f32[4,64,128]{2,1,0:T(8,128)S(1)} %fusion.83), channel_id=1, source_target_pairs={{0,8},{8,16},{16,24},{24,32},{32,40},{40,48},{48,56},{56,64},{64,7... | collective-permute-start | bytes 393224 | tf_op jit(solution)/shard_map/while/body/eval_jaxpr/ppermute | solution.py:15
  286.6 8.1 %collective-permute-start = (f32[4,64,128]{2,1,0:T(8,128)S(1)}, f32[4,64,128]{2,1,0:T(8,128)S(1)}, u32[]{:S(2)}, u32[]{:S(2)}) collective-permute-start(f32[4,64,128]{2,1,0:T(8,128)S(1)} %fusion.82), channel_id=1, source_target_pairs={{0,8},{8,16},{16,24},{24,32},{32,40},{40,48},{48,56},{56,64},{64,7... | collective-permute-start | bytes 393224 | tf_op jit(solution)/shard_map/while/body/eval_jaxpr/ppermute | solution.py:15
  287.0 9.1 %collective-permute-start.1 = (f32[4,64,128]{2,1,0:T(8,128)S(1)}, f32[4,64,128]{2,1,0:T(8,128)S(1)}, u32[]{:S(2)}, u32[]{:S(2)}) collective-permute-start(f32[4,64,128]{2,1,0:T(8,128)S(1)} %fusion.83), channel_id=1, source_target_pairs={{0,8},{8,16},{16,24},{24,32},{32,40},{40,48},{48,56},{56,64},{64,7... | collective-permute-start | bytes 393224 | tf_op jit(solution)/shard_map/while/body/eval_jaxpr/ppermute | solution.py:15
  299.6 8.1 %collective-permute-start = (f32[4,64,128]{2,1,0:T(8,128)S(1)}, f32[4,64,128]{2,1,0:T(8,128)S(1)}, u32[]{:S(2)}, u32[]{:S(2)}) collective-permute-start(f32[4,64,128]{2,1,0:T(8,128)S(1)} %fusion.82), channel_id=1, source_target_pairs={{0,8},{8,16},{16,24},{24,32},{32,40},{40,48},{48,56},{56,64},{64,7... | collective-permute-start | bytes 393224 | tf_op jit(solution)/shard_map/while/body/eval_jaxpr/ppermute | solution.py:15
  300.0 9.1 %collective-permute-start.1 = (f32[4,64,128]{2,1,0:T(8,128)S(1)}, f32[4,64,128]{2,1,0:T(8,128)S(1)}, u32[]{:S(2)}, u32[]{:S(2)}) collective-permute-start(f32[4,64,128]{2,1,0:T(8,128)S(1)} %fusion.83), channel_id=1, source_target_pairs={{0,8},{8,16},{16,24},{24,32},{32,40},{40,48},{48,56},{56,64},{64,7... | collective-permute-start | bytes 393224 | tf_op jit(solution)/shard_map/while/body/eval_jaxpr/ppermute | solution.py:15
  312.6 8.1 %collective-permute-start = (f32[4,64,128]{2,1,0:T(8,128)S(1)}, f32[4,64,128]{2,1,0:T(8,128)S(1)}, u32[]{:S(2)}, u32[]{:S(2)}) collective-permute-start(f32[4,64,128]{2,1,0:T(8,128)S(1)} %fusion.82), channel_id=1, source_target_pairs={{0,8},{8,16},{16,24},{24,32},{32,40},{40,48},{48,56},{56,64},{64,7... | collective-permute-start | bytes 393224 | tf_op jit(solution)/shard_map/while/body/eval_jaxpr/ppermute | solution.py:15
  312.9 9.1 %collective-permute-start.1 = (f32[4,64,128]{2,1,0:T(8,128)S(1)}, f32[4,64,128]{2,1,0:T(8,128)S(1)}, u32[]{:S(2)}, u32[]{:S(2)}) collective-permute-start(f32[4,64,128]{2,1,0:T(8,128)S(1)} %fusion.83), channel_id=1, source_target_pairs={{0,8},{8,16},{16,24},{24,32},{32,40},{40,48},{48,56},{56,64},{64,7... | collective-permute-start | bytes 393224 | tf_op jit(solution)/shard_map/while/body/eval_jaxpr/ppermute | solution.py:15
  325.5 8.1 %collective-permute-start = (f32[4,64,128]{2,1,0:T(8,128)S(1)}, f32[4,64,128]{2,1,0:T(8,128)S(1)}, u32[]{:S(2)}, u32[]{:S(2)}) collective-permute-start(f32[4,64,128]{2,1,0:T(8,128)S(1)} %fusion.82), channel_id=1, source_target_pairs={{0,8},{8,16},{16,24},{24,32},{32,40},{40,48},{48,56},{56,64},{64,7... | collective-permute-start | bytes 393224 | tf_op jit(solution)/shard_map/while/body/eval_jaxpr/ppermute | solution.py:15
  325.9 9.1 %collective-permute-start.1 = (f32[4,64,128]{2,1,0:T(8,128)S(1)}, f32[4,64,128]{2,1,0:T(8,128)S(1)}, u32[]{:S(2)}, u32[]{:S(2)}) collective-permute-start(f32[4,64,128]{2,1,0:T(8,128)S(1)} %fusion.83), channel_id=1, source_target_pairs={{0,8},{8,16},{16,24},{24,32},{32,40},{40,48},{48,56},{56,64},{64,7... | collective-permute-start | bytes 393224 | tf_op jit(solution)/shard_map/while/body/eval_jaxpr/ppermute | solution.py:15
  338.5 8.1 %collective-permute-start = (f32[4,64,128]{2,1,0:T(8,128)S(1)}, f32[4,64,128]{2,1,0:T(8,128)S(1)}, u32[]{:S(2)}, u32[]{:S(2)}) collective-permute-start(f32[4,64,128]{2,1,0:T(8,128)S(1)} %fusion.82), channel_id=1, source_target_pairs={{0,8},{8,16},{16,24},{24,32},{32,40},{40,48},{48,56},{56,64},{64,7... | collective-permute-start | bytes 393224 | tf_op jit(solution)/shard_map/while/body/eval_jaxpr/ppermute | solution.py:15
  338.9 9.1 %collective-permute-start.1 = (f32[4,64,128]{2,1,0:T(8,128)S(1)}, f32[4,64,128]{2,1,0:T(8,128)S(1)}, u32[]{:S(2)}, u32[]{:S(2)}) collective-permute-start(f32[4,64,128]{2,1,0:T(8,128)S(1)} %fusion.83), channel_id=1, source_target_pairs={{0,8},{8,16},{16,24},{24,32},{32,40},{40,48},{48,56},{56,64},{64,7... | collective-permute-start | bytes 393224 | tf_op jit(solution)/shard_map/while/body/eval_jaxpr/ppermute | solution.py:15
  351.5 8.1 %collective-permute-start = (f32[4,64,128]{2,1,0:T(8,128)S(1)}, f32[4,64,128]{2,1,0:T(8,128)S(1)}, u32[]{:S(2)}, u32[]{:S(2)}) collective-permute-start(f32[4,64,128]{2,1,0:T(8,128)S(1)} %fusion.82), channel_id=1, source_target_pairs={{0,8},{8,16},{16,24},{24,32},{32,40},{40,48},{48,56},{56,64},{64,7... | collective-permute-start | bytes 393224 | tf_op jit(solution)/shard_map/while/body/eval_jaxpr/ppermute | solution.py:15
  351.9 9.1 %collective-permute-start.1 = (f32[4,64,128]{2,1,0:T(8,128)S(1)}, f32[4,64,128]{2,1,0:T(8,128)S(1)}, u32[]{:S(2)}, u32[]{:S(2)}) collective-permute-start(f32[4,64,128]{2,1,0:T(8,128)S(1)} %fusion.83), channel_id=1, source_target_pairs={{0,8},{8,16},{16,24},{24,32},{32,40},{40,48},{48,56},{56,64},{64,7... | collective-permute-start | bytes 393224 | tf_op jit(solution)/shard_map/while/body/eval_jaxpr/ppermute | solution.py:15
  364.5 8.1 %collective-permute-start = (f32[4,64,128]{2,1,0:T(8,128)S(1)}, f32[4,64,128]{2,1,0:T(8,128)S(1)}, u32[]{:S(2)}, u32[]{:S(2)}) collective-permute-start(f32[4,64,128]{2,1,0:T(8,128)S(1)} %fusion.82), channel_id=1, source_target_pairs={{0,8},{8,16},{16,24},{24,32},{32,40},{40,48},{48,56},{56,64},{64,7... | collective-permute-start | bytes 393224 | tf_op jit(solution)/shard_map/while/body/eval_jaxpr/ppermute | solution.py:15
  364.8 9.1 %collective-permute-start.1 = (f32[4,64,128]{2,1,0:T(8,128)S(1)}, f32[4,64,128]{2,1,0:T(8,128)S(1)}, u32[]{:S(2)}, u32[]{:S(2)}) collective-permute-start(f32[4,64,128]{2,1,0:T(8,128)S(1)} %fusion.83), channel_id=1, source_target_pairs={{0,8},{8,16},{16,24},{24,32},{32,40},{40,48},{48,56},{56,64},{64,7... | collective-permute-start | bytes 393224 | tf_op jit(solution)/shard_map/while/body/eval_jaxpr/ppermute | solution.py:15
  377.4 8.1 %collective-permute-start = (f32[4,64,128]{2,1,0:T(8,128)S(1)}, f32[4,64,128]{2,1,0:T(8,128)S(1)}, u32[]{:S(2)}, u32[]{:S(2)}) collective-permute-start(f32[4,64,128]{2,1,0:T(8,128)S(1)} %fusion.82), channel_id=1, source_target_pairs={{0,8},{8,16},{16,24},{24,32},{32,40},{40,48},{48,56},{56,64},{64,7... | collective-permute-start | bytes 393224 | tf_op jit(solution)/shard_map/while/body/eval_jaxpr/ppermute | solution.py:15
  377.8 9.1 %collective-permute-start.1 = (f32[4,64,128]{2,1,0:T(8,128)S(1)}, f32[4,64,128]{2,1,0:T(8,128)S(1)}, u32[]{:S(2)}, u32[]{:S(2)}) collective-permute-start(f32[4,64,128]{2,1,0:T(8,128)S(1)} %fusion.83), channel_id=1, source_target_pairs={{0,8},{8,16},{16,24},{24,32},{32,40},{40,48},{48,56},{56,64},{64,7... | collective-permute-start | bytes 393224 | tf_op jit(solution)/shard_map/while/body/eval_jaxpr/ppermute | solution.py:15
  390.4 8.1 %collective-permute-start = (f32[4,64,128]{2,1,0:T(8,128)S(1)}, f32[4,64,128]{2,1,0:T(8,128)S(1)}, u32[]{:S(2)}, u32[]{:S(2)}) collective-permute-start(f32[4,64,128]{2,1,0:T(8,128)S(1)} %fusion.82), channel_id=1, source_target_pairs={{0,8},{8,16},{16,24},{24,32},{32,40},{40,48},{48,56},{56,64},{64,7... | collective-permute-start | bytes 393224 | tf_op jit(solution)/shard_map/while/body/eval_jaxpr/ppermute | solution.py:15
  390.8 9.1 %collective-permute-start.1 = (f32[4,64,128]{2,1,0:T(8,128)S(1)}, f32[4,64,128]{2,1,0:T(8,128)S(1)}, u32[]{:S(2)}, u32[]{:S(2)}) collective-permute-start(f32[4,64,128]{2,1,0:T(8,128)S(1)} %fusion.83), channel_id=1, source_target_pairs={{0,8},{8,16},{16,24},{24,32},{32,40},{40,48},{48,56},{56,64},{64,7... | collective-permute-start | bytes 393224 | tf_op jit(solution)/shard_map/while/body/eval_jaxpr/ppermute | solution.py:15
  403.4 8.1 %collective-permute-start = (f32[4,64,128]{2,1,0:T(8,128)S(1)}, f32[4,64,128]{2,1,0:T(8,128)S(1)}, u32[]{:S(2)}, u32[]{:S(2)}) collective-permute-start(f32[4,64,128]{2,1,0:T(8,128)S(1)} %fusion.82), channel_id=1, source_target_pairs={{0,8},{8,16},{16,24},{24,32},{32,40},{40,48},{48,56},{56,64},{64,7... | collective-permute-start | bytes 393224 | tf_op jit(solution)/shard_map/while/body/eval_jaxpr/ppermute | solution.py:15
  403.8 9.1 %collective-permute-start.1 = (f32[4,64,128]{2,1,0:T(8,128)S(1)}, f32[4,64,128]{2,1,0:T(8,128)S(1)}, u32[]{:S(2)}, u32[]{:S(2)}) collective-permute-start(f32[4,64,128]{2,1,0:T(8,128)S(1)} %fusion.83), channel_id=1, source_target_pairs={{0,8},{8,16},{16,24},{24,32},{32,40},{40,48},{48,56},{56,64},{64,7... | collective-permute-start | bytes 393224 | tf_op jit(solution)/shard_map/while/body/eval_jaxpr/ppermute | solution.py:15
  416.4 8.1 %collective-permute-start = (f32[4,64,128]{2,1,0:T(8,128)S(1)}, f32[4,64,128]{2,1,0:T(8,128)S(1)}, u32[]{:S(2)}, u32[]{:S(2)}) collective-permute-start(f32[4,64,128]{2,1,0:T(8,128)S(1)} %fusion.82), channel_id=1, source_target_pairs={{0,8},{8,16},{16,24},{24,32},{32,40},{40,48},{48,56},{56,64},{64,7... | collective-permute-start | bytes 393224 | tf_op jit(solution)/shard_map/while/body/eval_jaxpr/ppermute | solution.py:15
  416.7 9.1 %collective-permute-start.1 = (f32[4,64,128]{2,1,0:T(8,128)S(1)}, f32[4,64,128]{2,1,0:T(8,128)S(1)}, u32[]{:S(2)}, u32[]{:S(2)}) collective-permute-start(f32[4,64,128]{2,1,0:T(8,128)S(1)} %fusion.83), channel_id=1, source_target_pairs={{0,8},{8,16},{16,24},{24,32},{32,40},{40,48},{48,56},{56,64},{64,7... | collective-permute-start | bytes 393224 | tf_op jit(solution)/shard_map/while/body/eval_jaxpr/ppermute | solution.py:15
  429.3 8.1 %collective-permute-start = (f32[4,64,128]{2,1,0:T(8,128)S(1)}, f32[4,64,128]{2,1,0:T(8,128)S(1)}, u32[]{:S(2)}, u32[]{:S(2)}) collective-permute-start(f32[4,64,128]{2,1,0:T(8,128)S(1)} %fusion.82), channel_id=1, source_target_pairs={{0,8},{8,16},{16,24},{24,32},{32,40},{40,48},{48,56},{56,64},{64,7... | collective-permute-start | bytes 393224 | tf_op jit(solution)/shard_map/while/body/eval_jaxpr/ppermute | solution.py:15
  429.7 9.1 %collective-permute-start.1 = (f32[4,64,128]{2,1,0:T(8,128)S(1)}, f32[4,64,128]{2,1,0:T(8,128)S(1)}, u32[]{:S(2)}, u32[]{:S(2)}) collective-permute-start(f32[4,64,128]{2,1,0:T(8,128)S(1)} %fusion.83), channel_id=1, source_target_pairs={{0,8},{8,16},{16,24},{24,32},{32,40},{40,48},{48,56},{56,64},{64,7... | collective-permute-start | bytes 393224 | tf_op jit(solution)/shard_map/while/body/eval_jaxpr/ppermute | solution.py:15
  442.3 8.1 %collective-permute-start = (f32[4,64,128]{2,1,0:T(8,128)S(1)}, f32[4,64,128]{2,1,0:T(8,128)S(1)}, u32[]{:S(2)}, u32[]{:S(2)}) collective-permute-start(f32[4,64,128]{2,1,0:T(8,128)S(1)} %fusion.82), channel_id=1, source_target_pairs={{0,8},{8,16},{16,24},{24,32},{32,40},{40,48},{48,56},{56,64},{64,7... | collective-permute-start | bytes 393224 | tf_op jit(solution)/shard_map/while/body/eval_jaxpr/ppermute | solution.py:15
  442.7 9.1 %collective-permute-start.1 = (f32[4,64,128]{2,1,0:T(8,128)S(1)}, f32[4,64,128]{2,1,0:T(8,128)S(1)}, u32[]{:S(2)}, u32[]{:S(2)}) collective-permute-start(f32[4,64,128]{2,1,0:T(8,128)S(1)} %fusion.83), channel_id=1, source_target_pairs={{0,8},{8,16},{16,24},{24,32},{32,40},{40,48},{48,56},{56,64},{64,7... | collective-permute-start | bytes 393224 | tf_op jit(solution)/shard_map/while/body/eval_jaxpr/ppermute | solution.py:15
  455.3 8.1 %collective-permute-start = (f32[4,64,128]{2,1,0:T(8,128)S(1)}, f32[4,64,128]{2,1,0:T(8,128)S(1)}, u32[]{:S(2)}, u32[]{:S(2)}) collective-permute-start(f32[4,64,128]{2,1,0:T(8,128)S(1)} %fusion.82), channel_id=1, source_target_pairs={{0,8},{8,16},{16,24},{24,32},{32,40},{40,48},{48,56},{56,64},{64,7... | collective-permute-start | bytes 393224 | tf_op jit(solution)/shard_map/while/body/eval_jaxpr/ppermute | solution.py:15
  455.7 9.1 %collective-permute-start.1 = (f32[4,64,128]{2,1,0:T(8,128)S(1)}, f32[4,64,128]{2,1,0:T(8,128)S(1)}, u32[]{:S(2)}, u32[]{:S(2)}) collective-permute-start(f32[4,64,128]{2,1,0:T(8,128)S(1)} %fusion.83), channel_id=1, source_target_pairs={{0,8},{8,16},{16,24},{24,32},{32,40},{40,48},{48,56},{56,64},{64,7... | collective-permute-start | bytes 393224 | tf_op jit(solution)/shard_map/while/body/eval_jaxpr/ppermute | solution.py:15
  468.3 8.1 %collective-permute-start = (f32[4,64,128]{2,1,0:T(8,128)S(1)}, f32[4,64,128]{2,1,0:T(8,128)S(1)}, u32[]{:S(2)}, u32[]{:S(2)}) collective-permute-start(f32[4,64,128]{2,1,0:T(8,128)S(1)} %fusion.82), channel_id=1, source_target_pairs={{0,8},{8,16},{16,24},{24,32},{32,40},{40,48},{48,56},{56,64},{64,7... | collective-permute-start | bytes 393224 | tf_op jit(solution)/shard_map/while/body/eval_jaxpr/ppermute | solution.py:15
  468.7 9.1 %collective-permute-start.1 = (f32[4,64,128]{2,1,0:T(8,128)S(1)}, f32[4,64,128]{2,1,0:T(8,128)S(1)}, u32[]{:S(2)}, u32[]{:S(2)}) collective-permute-start(f32[4,64,128]{2,1,0:T(8,128)S(1)} %fusion.83), channel_id=1, source_target_pairs={{0,8},{8,16},{16,24},{24,32},{32,40},{40,48},{48,56},{56,64},{64,7... | collective-permute-start | bytes 393224 | tf_op jit(solution)/shard_map/while/body/eval_jaxpr/ppermute | solution.py:15
  481.2 8.1 %collective-permute-start = (f32[4,64,128]{2,1,0:T(8,128)S(1)}, f32[4,64,128]{2,1,0:T(8,128)S(1)}, u32[]{:S(2)}, u32[]{:S(2)}) collective-permute-start(f32[4,64,128]{2,1,0:T(8,128)S(1)} %fusion.82), channel_id=1, source_target_pairs={{0,8},{8,16},{16,24},{24,32},{32,40},{40,48},{48,56},{56,64},{64,7... | collective-permute-start | bytes 393224 | tf_op jit(solution)/shard_map/while/body/eval_jaxpr/ppermute | solution.py:15
  481.6 9.1 %collective-permute-start.1 = (f32[4,64,128]{2,1,0:T(8,128)S(1)}, f32[4,64,128]{2,1,0:T(8,128)S(1)}, u32[]{:S(2)}, u32[]{:S(2)}) collective-permute-start(f32[4,64,128]{2,1,0:T(8,128)S(1)} %fusion.83), channel_id=1, source_target_pairs={{0,8},{8,16},{16,24},{24,32},{32,40},{40,48},{48,56},{56,64},{64,7... | collective-permute-start | bytes 393224 | tf_op jit(solution)/shard_map/while/body/eval_jaxpr/ppermute | solution.py:15
  494.2 8.1 %collective-permute-start = (f32[4,64,128]{2,1,0:T(8,128)S(1)}, f32[4,64,128]{2,1,0:T(8,128)S(1)}, u32[]{:S(2)}, u32[]{:S(2)}) collective-permute-start(f32[4,64,128]{2,1,0:T(8,128)S(1)} %fusion.82), channel_id=1, source_target_pairs={{0,8},{8,16},{16,24},{24,32},{32,40},{40,48},{48,56},{56,64},{64,7... | collective-permute-start | bytes 393224 | tf_op jit(solution)/shard_map/while/body/eval_jaxpr/ppermute | solution.py:15
  494.6 9.1 %collective-permute-start.1 = (f32[4,64,128]{2,1,0:T(8,128)S(1)}, f32[4,64,128]{2,1,0:T(8,128)S(1)}, u32[]{:S(2)}, u32[]{:S(2)}) collective-permute-start(f32[4,64,128]{2,1,0:T(8,128)S(1)} %fusion.83), channel_id=1, source_target_pairs={{0,8},{8,16},{16,24},{24,32},{32,40},{40,48},{48,56},{56,64},{64,7... | collective-permute-start | bytes 393224 | tf_op jit(solution)/shard_map/while/body/eval_jaxpr/ppermute | solution.py:15
  507.2 8.1 %collective-permute-start = (f32[4,64,128]{2,1,0:T(8,128)S(1)}, f32[4,64,128]{2,1,0:T(8,128)S(1)}, u32[]{:S(2)}, u32[]{:S(2)}) collective-permute-start(f32[4,64,128]{2,1,0:T(8,128)S(1)} %fusion.82), channel_id=1, source_target_pairs={{0,8},{8,16},{16,24},{24,32},{32,40},{40,48},{48,56},{56,64},{64,7... | collective-permute-start | bytes 393224 | tf_op jit(solution)/shard_map/while/body/eval_jaxpr/ppermute | solution.py:15
  507.6 9.1 %collective-permute-start.1 = (f32[4,64,128]{2,1,0:T(8,128)S(1)}, f32[4,64,128]{2,1,0:T(8,128)S(1)}, u32[]{:S(2)}, u32[]{:S(2)}) collective-permute-start(f32[4,64,128]{2,1,0:T(8,128)S(1)} %fusion.83), channel_id=1, source_target_pairs={{0,8},{8,16},{16,24},{24,32},{32,40},{40,48},{48,56},{56,64},{64,7... | collective-permute-start | bytes 393224 | tf_op jit(solution)/shard_map/while/body/eval_jaxpr/ppermute | solution.py:15
  520.2 8.1 %collective-permute-start = (f32[4,64,128]{2,1,0:T(8,128)S(1)}, f32[4,64,128]{2,1,0:T(8,128)S(1)}, u32[]{:S(2)}, u32[]{:S(2)}) collective-permute-start(f32[4,64,128]{2,1,0:T(8,128)S(1)} %fusion.82), channel_id=1, source_target_pairs={{0,8},{8,16},{16,24},{24,32},{32,40},{40,48},{48,56},{56,64},{64,7... | collective-permute-start | bytes 393224 | tf_op jit(solution)/shard_map/while/body/eval_jaxpr/ppermute | solution.py:15
  520.6 9.1 %collective-permute-start.1 = (f32[4,64,128]{2,1,0:T(8,128)S(1)}, f32[4,64,128]{2,1,0:T(8,128)S(1)}, u32[]{:S(2)}, u32[]{:S(2)}) collective-permute-start(f32[4,64,128]{2,1,0:T(8,128)S(1)} %fusion.83), channel_id=1, source_target_pairs={{0,8},{8,16},{16,24},{24,32},{32,40},{40,48},{48,56},{56,64},{64,7... | collective-permute-start | bytes 393224 | tf_op jit(solution)/shard_map/while/body/eval_jaxpr/ppermute | solution.py:15
  533.5 9.1 %collective-permute-start.1 = (f32[4,64,128]{2,1,0:T(8,128)S(1)}, f32[4,64,128]{2,1,0:T(8,128)S(1)}, u32[]{:S(2)}, u32[]{:S(2)}) collective-permute-start(f32[4,64,128]{2,1,0:T(8,128)S(1)} %fusion.83), channel_id=1, source_target_pairs={{0,8},{8,16},{16,24},{24,32},{32,40},{40,48},{48,56},{56,64},{64,7... | collective-permute-start | bytes 393224 | tf_op jit(solution)/shard_map/while/body/eval_jaxpr/ppermute | solution.py:15
  546.5 9.1 %collective-permute-start.1 = (f32[4,64,128]{2,1,0:T(8,128)S(1)}, f32[4,64,128]{2,1,0:T(8,128)S(1)}, u32[]{:S(2)}, u32[]{:S(2)}) collective-permute-start(f32[4,64,128]{2,1,0:T(8,128)S(1)} %fusion.83), channel_id=1, source_target_pairs={{0,8},{8,16},{16,24},{24,32},{32,40},{40,48},{48,56},{56,64},{64,7... | collective-permute-start | bytes 393224 | tf_op jit(solution)/shard_map/while/body/eval_jaxpr/ppermute | solution.py:15
  559.5 9.1 %collective-permute-start.1 = (f32[4,64,128]{2,1,0:T(8,128)S(1)}, f32[4,64,128]{2,1,0:T(8,128)S(1)}, u32[]{:S(2)}, u32[]{:S(2)}) collective-permute-start(f32[4,64,128]{2,1,0:T(8,128)S(1)} %fusion.83), channel_id=1, source_target_pairs={{0,8},{8,16},{16,24},{24,32},{32,40},{40,48},{48,56},{56,64},{64,7... | collective-permute-start | bytes 393224 | tf_op jit(solution)/shard_map/while/body/eval_jaxpr/ppermute | solution.py:15
  572.5 9.1 %collective-permute-start.1 = (f32[4,64,128]{2,1,0:T(8,128)S(1)}, f32[4,64,128]{2,1,0:T(8,128)S(1)}, u32[]{:S(2)}, u32[]{:S(2)}) collective-permute-start(f32[4,64,128]{2,1,0:T(8,128)S(1)} %fusion.83), channel_id=1, source_target_pairs={{0,8},{8,16},{16,24},{24,32},{32,40},{40,48},{48,56},{56,64},{64,7... | collective-permute-start | bytes 393224 | tf_op jit(solution)/shard_map/while/body/eval_jaxpr/ppermute | solution.py:15
  585.4 9.1 %collective-permute-start.1 = (f32[4,64,128]{2,1,0:T(8,128)S(1)}, f32[4,64,128]{2,1,0:T(8,128)S(1)}, u32[]{:S(2)}, u32[]{:S(2)}) collective-permute-start(f32[4,64,128]{2,1,0:T(8,128)S(1)} %fusion.83), channel_id=1, source_target_pairs={{0,8},{8,16},{16,24},{24,32},{32,40},{40,48},{48,56},{56,64},{64,7... | collective-permute-start | bytes 393224 | tf_op jit(solution)/shard_map/while/body/eval_jaxpr/ppermute | solution.py:15
  598.0 8.1 %collective-permute-start = (f32[4,64,128]{2,1,0:T(8,128)S(1)}, f32[4,64,128]{2,1,0:T(8,128)S(1)}, u32[]{:S(2)}, u32[]{:S(2)}) collective-permute-start(f32[4,64,128]{2,1,0:T(8,128)S(1)} %fusion.82), channel_id=1, source_target_pairs={{0,8},{8,16},{16,24},{24,32},{32,40},{40,48},{48,56},{56,64},{64,7... | collective-permute-start | bytes 393224 | tf_op jit(solution)/shard_map/while/body/eval_jaxpr/ppermute | solution.py:15
  598.4 9.1 %collective-permute-start.1 = (f32[4,64,128]{2,1,0:T(8,128)S(1)}, f32[4,64,128]{2,1,0:T(8,128)S(1)}, u32[]{:S(2)}, u32[]{:S(2)}) collective-permute-start(f32[4,64,128]{2,1,0:T(8,128)S(1)} %fusion.83), channel_id=1, source_target_pairs={{0,8},{8,16},{16,24},{24,32},{32,40},{40,48},{48,56},{56,64},{64,7... | collective-permute-start | bytes 393224 | tf_op jit(solution)/shard_map/while/body/eval_jaxpr/ppermute | solution.py:15
  608.3 11.0 %all-to-all-start.3 = ((bf16[4,64,128]{2,0,1:T(4,128)(2,1)}), bf16[4,64,128]{2,0,1:T(4,128)(2,1)S(1)}, u32[]{:S(2)}, u32[]{:S(2)}) async-start(bf16[4,64,128]{2,0,1:T(4,128)(2,1)} %copy.80), calls=%async_computation.3 | async-start | bytes 131072 | tf_op jit(solution)/shard_map/all_to_all | solution.py:148
  619.3 10.6 %all-to-all-start.2 = ((bf16[4,64,128]{2,0,1:T(4,128)(2,1)}), bf16[4,64,128]{2,0,1:T(4,128)(2,1)S(1)}, u32[]{:S(2)}, u32[]{:S(2)}) async-start(bf16[4,64,128]{2,0,1:T(4,128)(2,1)} %copy.81), calls=%async_computation.2 | async-start | bytes 131072 | tf_op jit(solution)/shard_map/all_to_all | solution.py:147
  629.9 11.6 %all-to-all-start.1 = ((bf16[4,64,1024]{2,0,1:T(4,128)(2,1)}), bf16[4,64,1024]{2,0,1:T(4,128)(2,1)S(1)}, u32[]{:S(2)}, u32[]{:S(2)}) async-start(bf16[4,64,1024]{2,0,1:T(4,128)(2,1)} %reshape.196), calls=%async_computation.1 | async-start | bytes 1048576 | tf_op jit(solution)/shard_map/all_to_all | solution.py:146
  (13 other events, 190.0 us)
Sparse Core Ops, SparseCore 0:
  10.8 88.4 all-gather.3
